TPU v7x, 32 devices: a whole 2x2x4 slice. The times are simulated.
32 devices in a mesh: row: 4 (over x, core), col: 8 (over z, y).
Axes of the slice: x: 2, y: 2, z: 4, core: 2. Of those that a mesh axis runs over, the one named last changes fastest.
Arguments:
- density_factor: bfloat16 [131072, 256], P(('row', 'col'))
- onsite: float32 [131072], P(('row', 'col')), may hold values from -4 to 4
- neighbour_ids: int32 [256, 8], P(('row', 'col')), may hold values from 0 to 255, as said below
- neighbour_count: int32 [256], P(('row', 'col')), may hold values from 1 to 8, as said below
- coupling_type: int32 [256, 8], P(('row', 'col')), may hold values from 0 to 3
- coupling_blocks: bfloat16 [4, 512, 512], replicated, may hold values from -0.25 to 0.25
- bath_pattern: int32 [256], P(('row', 'col')), may hold values from 0 to 3
- bath_blocks: bfloat16 [4, 512, 512], replicated, may hold values from -0.25 to 0.25
Outputs:
- new_factor: bfloat16 [131072, 256], P(('row', 'col'))
Inputs may be any that keep to these rules, and one draw needn't show every extreme that they name: `neighbour_ids`: every neighbour of block b lies among the 64 blocks that share b's index of row, at most half of 64 blocks from b when that group is taken as a loop, and is never b itself; some block has a neighbour exactly half of 64 blocks away. Only the first neighbour_count[b] slots of block b's lists are used; some block uses all 8.
All inputs are finite; a program needn't handle non-finite values.
Results may differ from a plain program's by a relative error of at most 0.0056.
Values may be sent and summed in bfloat16 or wider, within the bound.
No kernel may reach another device: no remote copies, remote signals or barrier semaphores. Data moves between devices by JAX's collectives and lax.ppermute only.
A program may use at most 192 MiB of HBM per device.

v0:
```python
import jax
import jax.numpy as jnp
from jax import lax
from jax.experimental import pallas as pl
from jax.experimental.pallas import tpu as pltpu
from jax.sharding import PartitionSpec as P

SWEEPS = 2
time_step = 0.25
PANEL = 64
HIGHEST = lax.Precision.HIGHEST


def bath_kernel(pattern_ref, bath_ref, own_ref, bathed_ref, gram_ref):
    bathed = jnp.dot(bath_ref[0], own_ref[...], preferred_element_type=jnp.float32).astype(jnp.bfloat16)
    bathed_ref[...] = bathed
    part = lax.dot_general(
        bathed, bathed, (((0,), (0,)), ((), ())), preferred_element_type=jnp.float32
    )

    @pl.when(pl.program_id(0) == 0)
    def _():
        gram_ref[...] = part

    @pl.when(pl.program_id(0) > 0)
    def _():
        gram_ref[...] += part


def bath_part(own, bath_pattern, bath_blocks):
    blocks = bath_pattern.shape[0]
    block_rows = bath_blocks.shape[1]
    rows, rank = own.shape
    tile = pl.BlockSpec((block_rows, rank), lambda b, kind: (b, 0))
    return pl.pallas_call(
        bath_kernel,
        grid_spec=pltpu.PrefetchScalarGridSpec(
            num_scalar_prefetch=1,
            grid=(blocks,),
            in_specs=[
                pl.BlockSpec((1, block_rows, block_rows), lambda b, kind: (kind[b], 0, 0)),
                tile,
            ],
            out_specs=[tile, pl.BlockSpec((rank, rank), lambda b, kind: (0, 0))],
        ),
        out_shape=[
            jax.ShapeDtypeStruct((rows, rank), jnp.bfloat16),
            jax.ShapeDtypeStruct((rank, rank), jnp.float32),
        ],
        compiler_params=pltpu.CompilerParams(vmem_limit_bytes=12 * 2**20),
        name="bath",
    )(bath_pattern, bath_blocks, own)


def gather_products(origin_ref, offset_ref, first_ref, count_ref, kind_ref, sources, coupling_ref, held, sems, total):
    blocks, slots = origin_ref.shape
    block_rows = held.shape[2]
    b = pl.program_id(0)
    group = 1
    while group * group < len(sources):
        group += 1

    def copy(source, block, slot):
        start = pl.multiple_of(offset_ref[block, slot] * block_rows, block_rows)
        return pltpu.make_async_copy(
            source.at[pl.ds(start, block_rows), :],
            held.at[lax.rem(block, 2), slot],
            sems.at[lax.rem(block, 2), slot],
        )

    def fetch(block):
        def one(slot, carry):
            origin = origin_ref[block, slot]
            for low in range(0, len(sources), group):
                high = min(low + group, len(sources))

                @pl.when((origin >= low) & (origin < high))
                def _():
                    for place in range(low, high):
                        @pl.when(origin == place)
                        def _():
                            copy(sources[place], block, slot).start()
            return carry

        lax.fori_loop(first_ref[block], first_ref[block] + count_ref[block], one, 0)

    @pl.when(b == 0)
    def _():
        fetch(0)

    @pl.when(b + 1 < blocks)
    def _():
        fetch(b + 1)

    def add(slot, carry):
        copy(sources[0], b, slot).wait()
        total[...] -= time_step * jnp.dot(
            coupling_ref[kind_ref[b, slot]],
            held[lax.rem(b, 2), slot],
            preferred_element_type=jnp.float32,
        )
        return carry

    lax.fori_loop(first_ref[b], first_ref[b] + count_ref[b], add, 0)


def early_kernel(origin_ref, offset_ref, first_ref, count_ref, kind_ref, *refs):
    sources = refs[:-6]
    coupling_ref, own_ref, energy_ref, total_ref, held, sems = refs[-6:]
    block_rows = own_ref.shape[0]
    row = energy_ref[pl.ds(pl.program_id(0), 1), :]
    energy = jnp.broadcast_to(row, (8, block_rows)).T[:, :1]
    wide = own_ref[...].astype(jnp.float32)
    total_ref[...] = wide - time_step * (energy * wide)
    gather_products(
        origin_ref, offset_ref, first_ref, count_ref, kind_ref, sources, coupling_ref, held, sems, total_ref
    )


def late_kernel(origin_ref, offset_ref, first_ref, count_ref, kind_ref, *refs):
    sources = refs[:-8]
    coupling_ref, base_ref, bathed_ref, moved_ref, gram_ref, total, held, sems = refs[-8:]
    b = pl.program_id(0)
    total[...] = base_ref[...]
    gather_products(
        origin_ref, offset_ref, first_ref, count_ref, kind_ref, sources, coupling_ref, held, sems, total
    )
    moved = total[...].astype(jnp.bfloat16)
    moved_ref[...] = moved
    both = jnp.concatenate([moved, bathed_ref[...]], axis=1)
    part = lax.dot_general(
        moved, both, (((0,), (0,)), ((), ())), preferred_element_type=jnp.float32
    )

    @pl.when(b == 0)
    def _():
        gram_ref[...] = part

    @pl.when(b > 0)
    def _():
        gram_ref[...] += part


def early_part(lists, sources, coupling_blocks, own, onsite):
    blocks, slots = lists[0].shape
    kinds, block_rows, _ = coupling_blocks.shape
    rows, rank = own.shape
    tile = pl.BlockSpec((block_rows, rank), lambda b, *_: (b, 0))
    return pl.pallas_call(
        early_kernel,
        grid_spec=pltpu.PrefetchScalarGridSpec(
            num_scalar_prefetch=5,
            grid=(blocks,),
            in_specs=[
                *[pl.BlockSpec(memory_space=pl.ANY) for _ in sources],
                pl.BlockSpec((kinds, block_rows, block_rows), lambda b, *_: (0, 0, 0)),
                tile,
                pl.BlockSpec((blocks, block_rows), lambda b, *_: (0, 0)),
            ],
            out_specs=tile,
            scratch_shapes=[
                pltpu.VMEM((2, slots, block_rows, rank), jnp.bfloat16),
                pltpu.SemaphoreType.DMA((2, slots)),
            ],
        ),
        out_shape=jax.ShapeDtypeStruct((rows, rank), jnp.float32),
        compiler_params=pltpu.CompilerParams(vmem_limit_bytes=16 * 2**20),
        cost_estimate=pl.CostEstimate(
            flops=blocks * slots * block_rows * block_rows * rank,
            bytes_accessed=blocks * slots * block_rows * rank * 2,
            transcendentals=0,
        ),
        name="couple_early",
    )(*lists, *sources, coupling_blocks, own, onsite.reshape(blocks, block_rows))


def late_part(lists, sources, coupling_blocks, base, bathed):
    blocks, slots = lists[0].shape
    kinds, block_rows, _ = coupling_blocks.shape
    rows, rank = base.shape
    tile = pl.BlockSpec((block_rows, rank), lambda b, *_: (b, 0))
    return pl.pallas_call(
        late_kernel,
        grid_spec=pltpu.PrefetchScalarGridSpec(
            num_scalar_prefetch=5,
            grid=(blocks,),
            in_specs=[
                *[pl.BlockSpec(memory_space=pl.ANY) for _ in sources],
                pl.BlockSpec((kinds, block_rows, block_rows), lambda b, *_: (0, 0, 0)),
                tile,
                tile,
            ],
            out_specs=[tile, pl.BlockSpec((rank, 2 * rank), lambda b, *_: (0, 0))],
            scratch_shapes=[
                pltpu.VMEM((block_rows, rank), jnp.float32),
                pltpu.VMEM((2, slots, block_rows, rank), jnp.bfloat16),
                pltpu.SemaphoreType.DMA((2, slots)),
            ],
        ),
        out_shape=[
            jax.ShapeDtypeStruct((rows, rank), jnp.bfloat16),
            jax.ShapeDtypeStruct((rank, 2 * rank), jnp.float32),
        ],
        compiler_params=pltpu.CompilerParams(vmem_limit_bytes=20 * 2**20),
        name="couple_late",
    )(*lists, *sources, coupling_blocks, base, bathed)


def inverse_factor(square):
    n = square.shape[0]
    eye = (
        lax.broadcasted_iota(jnp.int32, (n, n), 0) == lax.broadcasted_iota(jnp.int32, (n, n), 1)
    ).astype(jnp.float32)
    work = jnp.concatenate([square, eye], axis=1)
    bands = [work[8 * i : 8 * i + 8, :] for i in range(n // 8)]
    sublane = lax.broadcasted_iota(jnp.int32, (8, 2 * n), 0)
    out = []
    for g in range(n // 8):
        below = range(g, n // 8)
        columns = {
            i: [jnp.broadcast_to(bands[i][:, 8 * g + r : 8 * g + r + 1], (8, 2 * n)) for r in range(8)]
            for i in below
        }
        diagonal = jnp.zeros((8, 2 * n), jnp.float32)
        for r in range(8):
            pivots = [columns[g][q][r : r + 1, :] for q in range(r, 8)]
            scale = pl.reciprocal(pivots[0], approx=True)
            diagonal = jnp.where(sublane == r, columns[g][r], diagonal)
            row = bands[g][r : r + 1, :]
            for i in below:
                share = columns[i][r] * scale
                if i == g:
                    share = jnp.where(sublane > r, share, 0.0)
                for q in range(r + 1, 8):
                    columns[i][q] = columns[i][q] - share * pivots[q - r]
                bands[i] = bands[i] - share * row
        out.append(bands[g][:, n:] * lax.rsqrt(diagonal)[:, n:])
    return jnp.concatenate(out, axis=0)


def eliminate(inner, image):
    rank = inner.shape[0]

    def product(left, right, contract):
        return lax.dot_general(
            left, right, ((contract, (0,)), ((), ())),
            precision=HIGHEST, preferred_element_type=jnp.float32,
        )

    for low in range(0, rank, PANEL):
        high = low + PANEL
        here, first = low // 128 * 128, high // 128 * 128
        inverse = inverse_factor(inner[low:high, low:high])
        panel = product(inverse, inner[low:high, here:], (1,))
        inner[low:high, here:] = panel
        share = panel[:, high - here :]
        if high < rank:
            inner[high:, first:] -= product(share, panel[:, first - here :], (0,))
        side = product(inverse, image[low:high, :], (1,))
        image[low:high, :] = side
        if high < rank:
            image[high:, :] -= product(share, side, (0,))


def finish_kernel(
    order_ref, chunks_ref, moved_hbm, bathed_hbm, out_hbm,
    gram, inner, image, moved, bathed, out, in_sems, out_sems,
):
    rank = chunks_ref.shape[0]
    load_moved = pltpu.make_async_copy(moved_hbm, moved, in_sems.at[0])
    load_bathed = pltpu.make_async_copy(bathed_hbm, bathed, in_sems.at[1])
    load_moved.start()
    load_bathed.start()

    chunks = order_ref.shape[0]
    size = rank // chunks
    for i in range(chunks):
        rows = pl.ds(pl.multiple_of(order_ref[i] * size, size), size)
        chunk = chunks_ref[i * size : (i + 1) * size, :]
        gram[rows, :] = chunk[:, : 2 * rank]
        gram[pl.ds(pl.multiple_of(rank + order_ref[i] * size, size), size), rank:] = chunk[:, 2 * rank :]
    gram[rank:, :rank] = gram[:rank, rank:].T
    later = jnp.dot(gram[:rank, :], gram[...], precision=HIGHEST, preferred_element_type=jnp.float32)
    inner[...] = later[:, :rank]
    image[:, rank:] = later[:, rank:]
    for sweep in range(1, SWEEPS):
        eliminate(inner, image.at[:, rank:])
        upper = lax.broadcasted_iota(jnp.int32, (rank, rank), 0) <= lax.broadcasted_iota(jnp.int32, (rank, rank), 1)
        image[:, :rank] = jnp.where(upper, inner[...], 0.0)
        rows = image[...]
        inner[...] = lax.dot_general(
            rows, rows, (((1,), (1,)), ((), ())),
            precision=HIGHEST, preferred_element_type=jnp.float32,
        )
    eliminate(inner, image)
    rotation = image[...].astype(jnp.bfloat16)
    load_moved.wait()
    load_bathed.wait()
    pieces = out_sems.shape[0]
    size = moved.shape[0] // pieces

    def store(piece):
        rows = pl.ds(pl.multiple_of(piece * size, size), size)
        return pltpu.make_async_copy(out.at[rows, :], out_hbm.at[rows, :], out_sems.at[piece])

    def one(piece, carry):
        rows = pl.ds(pl.multiple_of(piece * size, size), size)
        value = lax.dot_general(
            moved[rows, :], rotation[:, :rank], (((1,), (1,)), ((), ())),
            preferred_element_type=jnp.float32,
        )
        value += lax.dot_general(
            bathed[rows, :], rotation[:, rank:], (((1,), (1,)), ((), ())),
            preferred_element_type=jnp.float32,
        )
        out[rows, :] = value.astype(jnp.bfloat16)
        store(piece).start()
        return carry

    lax.fori_loop(0, pieces, one, 0)

    def drain(piece, carry):
        store(piece).wait()
        return carry

    lax.fori_loop(0, pieces, drain, 0)


def finish_part(order, chunks, moved, bathed):
    rows, rank = moved.shape
    return pl.pallas_call(
        finish_kernel,
        in_specs=[
            pl.BlockSpec(memory_space=pltpu.SMEM),
            pl.BlockSpec(memory_space=pltpu.VMEM),
            pl.BlockSpec(memory_space=pl.ANY),
            pl.BlockSpec(memory_space=pl.ANY),
        ],
        out_specs=pl.BlockSpec(memory_space=pl.ANY),
        out_shape=jax.ShapeDtypeStruct((rows, rank), jnp.bfloat16),
        scratch_shapes=[
            pltpu.VMEM((2 * rank, 2 * rank), jnp.float32),
            pltpu.VMEM((rank, rank), jnp.float32),
            pltpu.VMEM((rank, 2 * rank), jnp.float32),
            pltpu.VMEM((rows, rank), jnp.bfloat16),
            pltpu.VMEM((rows, rank), jnp.bfloat16),
            pltpu.VMEM((rows, rank), jnp.bfloat16),
            pltpu.SemaphoreType.DMA((2,)),
            pltpu.SemaphoreType.DMA((8,)),
        ],
        compiler_params=pltpu.CompilerParams(vmem_limit_bytes=24 * 2**20),
        name="finish",
    )(order, chunks, moved, bathed)


def ring_order(count):
    wide = 2
    while 4 * wide * wide <= count:
        wide *= 2
    tall = count // wide
    walk = [0]
    for r in range(tall):
        across = range(1, wide)
        walk += [r * wide + c for c in (across if r % 2 == 0 else reversed(across))]
    return walk + [r * wide for r in range(tall - 1, 0, -1)]


PIECES = 4


def tie(one, other):
    return lax.optimization_barrier((one, other))


def ring_gather(own, side, stages):
    order = ring_order(lax.axis_size("col"))
    following = order[1:] + order[:1]
    forward = list(zip(order, following))
    back = list(zip(following, order))
    size = own.shape[0] // PIECES
    pieces = [own[i * size : (i + 1) * size] for i in range(PIECES)]
    stages = list(stages)
    steps = []
    for step in range(1, len(order)):
        if step > 1:
            pieces[-1], side = tie(pieces[-1], side)
        pieces = [
            lax.ppermute(piece, "col", forward if i < PIECES // 2 else back)
            for i, piece in enumerate(pieces)
        ]
        if step > 1 and stages:
            side = stages.pop(0)(side)
        steps.append(list(pieces))
    for stage in stages:
        side = stage(side)
    return steps, side


def slot_lists(ids, counts, kinds):
    blocks, slots = ids.shape
    count = lax.axis_size("col")
    order = ring_order(count)
    place = jnp.asarray([order.index(c) for c in range(count)], jnp.int32)
    col = jnp.arange(count, dtype=jnp.int32)
    mine = jnp.sum(jnp.where(col == lax.axis_index("col"), place, 0))
    owner, within = ids // blocks, ids % blocks
    theirs = jnp.sum(jnp.where(owner[..., None] == col, place, 0), axis=-1)
    in_piece = blocks // PIECES
    piece = within // in_piece
    step = jnp.where(piece >= PIECES // 2, theirs - mine, mine - theirs) % count
    last = step == count - 1
    origin = jnp.where(last, piece, jnp.where(step == 0, 0, 1 + (step - 1) * PIECES + piece))
    offset = jnp.where(step == 0, within, within % in_piece)
    slot = jnp.arange(slots, dtype=jnp.int32)
    used = slot[None, :] < counts[:, None]
    key = jnp.where(used, jnp.where(last, slots, 0), 2 * slots) + slot
    rank = jnp.sum((key[:, None, :] < key[:, :, None]).astype(jnp.int32), axis=-1)
    at = rank[:, :, None] == slot
    def arrange(values):
        return jnp.sum(jnp.where(at, values[:, :, None], 0), axis=1)

    late = jnp.sum((used & last).astype(jnp.int32), axis=1)
    early = counts - late
    origin, offset, kinds = arrange(origin), arrange(offset), arrange(kinds)
    return (origin, offset, jnp.zeros_like(early), early, kinds), (origin, offset, early, late, kinds)


def swap(value, axis, stride):
    count = lax.axis_size(axis)
    return lax.ppermute(value, axis, [(i, i ^ stride) for i in range(count)])


def strides(axis):
    return [1 << i for i in range(lax.axis_size(axis).bit_length() - 1)]


def halvings():
    return [("row", stride) for stride in strides("row")] + [("col", 1)]


def side_of(axis, stride):
    return (lax.axis_index(axis) // stride) % 2


def halve(value, axis, stride):
    half = value.shape[0] // 2
    upper = side_of(axis, stride)
    keep = lax.dynamic_slice_in_dim(value, upper * half, half, 0)
    give = lax.dynamic_slice_in_dim(value, (1 - upper) * half, half, 0)
    return keep + swap(give, axis, stride)


def halve_over_row(value):
    for stride in strides("row"):
        value = halve(value, "row", stride)
    return value


def sum_relative(value):
    value = halve(value, "col", 1)
    for stride in strides("col")[1:]:
        value = value + swap(value, "col", stride)
    for axis, stride in reversed(halvings()):
        value = jnp.concatenate([value, swap(value, axis, stride)], axis=0)
    return value


def chunk_order():
    swaps = halvings()
    order = []
    for relative in range(1 << len(swaps)):
        part = 0
        for i, (axis, stride) in enumerate(swaps):
            height = len(swaps) - 1 - i
            part = part + (side_of(axis, stride) ^ ((relative >> height) & 1)) * (1 << height)
        order.append(part)
    return jnp.stack(order).astype(jnp.int32)


def shards(
    density_factor,
    onsite,
    neighbour_ids,
    neighbour_count,
    coupling_type,
    coupling_blocks,
    bath_pattern,
    bath_blocks,
):
    blocks, slots = neighbour_ids.shape
    group_blocks = lax.axis_size("col") * blocks
    in_group = neighbour_ids - lax.axis_index("row") * group_blocks
    early, late = slot_lists(in_group, neighbour_count, coupling_type)
    bathed, corner = bath_part(density_factor, bath_pattern, bath_blocks)
    steps, corner = ring_gather(density_factor, corner, [halve_over_row])
    ready = [density_factor] + [piece for step in steps[:-1] for piece in step]
    total = early_part(early, ready, coupling_blocks, density_factor, onsite)
    moved, upper = late_part(late, steps[-1], coupling_blocks, total, bathed)
    gram = sum_relative(jnp.concatenate([halve_over_row(upper), corner], axis=1))
    return finish_part(chunk_order(), gram, moved, bathed)


def solution(mesh):
    placed = (
        P(("row", "col"), None),
        P(("row", "col")),
        P(("row", "col"), None),
        P(("row", "col")),
        P(("row", "col"), None),
        P(),
        P(("row", "col")),
        P(),
    )
    return jax.shard_map(
        shards, mesh=mesh, in_specs=placed, out_specs=P(("row", "col"), None), check_vma=False
    )
```

profile of v0, /device:TPU:0, one launch (start us, length us, event | category | flops | bytes accessed | tf_op | source)
XLA Modules:
  0.0 244.0 jit_solution(10490325179491846524)
XLA Ops:
  0.0 3.0 %fusion.10 = (bf16[1024,256]{1,0:T(8,128)(2,1)}, bf16[1024,256]{1,0:T(8,128)(2,1)}, bf16[1024,256]{1,0:T(8,128)(2,1)}, bf16[1024,256]{1,0:T(8,128)(2,1)}) fusion(bf16[4096,256]{1,0:T(8,128)(2,1)} %refs_26_.1), kind=kLoop, calls=%fused_computation.55 | loop fusion | bytes 4194304 | tf_op jit(solution)/shard_map/slice | solution.py:381
  3.0 3.0 %collective-permute-start.21 = (bf16[1024,256]{1,0:T(8,128)(2,1)}, bf16[1024,256]{1,0:T(8,128)(2,1)S(1)}, u32[]{:S(2)}, u32[]{:S(2)}) collective-permute-start(bf16[1024,256]{1,0:T(8,128)(2,1)} %get-tuple-element.42), channel_id=1, source_target_pairs={{1,0},{3,1},{5,3},{7,5},{6,7},{4,6},{2,4},{0,2},{9,8},{11,9},{13,1... | collective-permute-start | bytes 1572872 | tf_op jit(solution)/shard_map/ppermute | solution.py:388
  9.7 5.5 %bath.1 = (bf16[4096,256]{1,0:T(8,128)(2,1)S(1)}, f32[256,256]{1,0:T(8,128)S(1)}) custom-call(s32[8]{0:T(128)S(1)} %copy-done.21, bf16[4,512,512]{2,1,0:T(8,128)(2,1)S(1)} %copy-done.8, bf16[4096,256]{1,0:T(8,128)(2,1)S(1)} %copy-done), custom_call_target="tpu_custom_call" | custom-call | tf_op jit(solution)/shard_map/bath/pallas_call | solution.py:35
  16.5 2.5 %collective-permute-done.21.refs_4_ = bf16[1024,256]{1,0:T(8,128)(2,1)S(1)} collective-permute-done((bf16[1024,256]{1,0:T(8,128)(2,1)}, bf16[1024,256]{1,0:T(8,128)(2,1)S(1)}, u32[]{:S(2)}, u32[]{:S(2)}) %collective-permute-start.21) | collective-permute-done | bytes 524320 | tf_op jit(solution)/shard_map/ppermute | solution.py:388
  19.1 2.2 collective-permute-start.22
  21.3 9.0 %collective-permute-done.14.refs_3_ = bf16[1024,256]{1,0:T(8,128)(2,1)} collective-permute-done((bf16[1024,256]{1,0:T(8,128)(2,1)}, bf16[1024,256]{1,0:T(8,128)(2,1)}, u32[]{:S(2)}, u32[]{:S(2)}) %collective-permute-start.14) | collective-permute-done | bytes 524320 | tf_op jit(solution)/shard_map/ppermute | solution.py:388
  35.4 2.3 collective-permute-done.24
  37.7 3.8 %collective-permute-done.22.refs_8_ = bf16[1024,256]{1,0:T(8,128)(2,1)} collective-permute-done((bf16[1024,256]{1,0:T(8,128)(2,1)S(1)}, bf16[1024,256]{1,0:T(8,128)(2,1)}, u32[]{:S(2)}, u32[]{:S(2)}) %collective-permute-start.22) | collective-permute-done | bytes 524320 | tf_op jit(solution)/shard_map/ppermute | solution.py:388
  41.5 2.1 collective-permute-start.25
  43.7 9.1 %collective-permute-done.15.refs_7_ = bf16[1024,256]{1,0:T(8,128)(2,1)} collective-permute-done((bf16[1024,256]{1,0:T(8,128)(2,1)}, bf16[1024,256]{1,0:T(8,128)(2,1)}, u32[]{:S(2)}, u32[]{:S(2)}) %collective-permute-start.15) | collective-permute-done | bytes 524320 | tf_op jit(solution)/shard_map/ppermute | solution.py:388
  52.7 2.1 collective-permute-start.16
  54.9 9.0 %collective-permute-done.25.refs_12_ = bf16[1024,256]{1,0:T(8,128)(2,1)S(1)} collective-permute-done((bf16[1024,256]{1,0:T(8,128)(2,1)}, bf16[1024,256]{1,0:T(8,128)(2,1)S(1)}, u32[]{:S(2)}, u32[]{:S(2)}) %collective-permute-start.25) | collective-permute-done | bytes 524320 | tf_op jit(solution)/shard_map/ppermute | solution.py:388
  67.6 7.5 %collective-permute-done.16.refs_11_ = bf16[1024,256]{1,0:T(8,128)(2,1)S(1)} collective-permute-done((bf16[1024,256]{1,0:T(8,128)(2,1)}, bf16[1024,256]{1,0:T(8,128)(2,1)S(1)}, u32[]{:S(2)}, u32[]{:S(2)}) %collective-permute-start.16) | collective-permute-done | bytes 524320 | tf_op jit(solution)/shard_map/ppermute | solution.py:388
  78.9 7.6 %collective-permute-done.26.refs_16_ = bf16[1024,256]{1,0:T(8,128)(2,1)} collective-permute-done((bf16[1024,256]{1,0:T(8,128)(2,1)S(1)}, bf16[1024,256]{1,0:T(8,128)(2,1)}, u32[]{:S(2)}, u32[]{:S(2)}) %collective-permute-start.26) | collective-permute-done | bytes 524320 | tf_op jit(solution)/shard_map/ppermute | solution.py:388
  86.5 2.1 collective-permute-start.27
  88.6 9.1 %collective-permute-done.17.refs_15_ = bf16[1024,256]{1,0:T(8,128)(2,1)} collective-permute-done((bf16[1024,256]{1,0:T(8,128)(2,1)S(1)}, bf16[1024,256]{1,0:T(8,128)(2,1)}, u32[]{:S(2)}, u32[]{:S(2)}) %collective-permute-start.17) | collective-permute-done | bytes 524320 | tf_op jit(solution)/shard_map/ppermute | solution.py:388
  97.7 2.1 collective-permute-start.18
  100.2 8.8 %collective-permute-done.27.refs_20_ = bf16[1024,256]{1,0:T(8,128)(2,1)} collective-permute-done((bf16[1024,256]{1,0:T(8,128)(2,1)}, bf16[1024,256]{1,0:T(8,128)(2,1)}, u32[]{:S(2)}, u32[]{:S(2)}) %collective-permute-start.27) | collective-permute-done | bytes 524320 | tf_op jit(solution)/shard_map/ppermute | solution.py:388
  111.1 9.1 %collective-permute-done.18.refs_19_ = bf16[1024,256]{1,0:T(8,128)(2,1)} collective-permute-done((bf16[1024,256]{1,0:T(8,128)(2,1)}, bf16[1024,256]{1,0:T(8,128)(2,1)}, u32[]{:S(2)}, u32[]{:S(2)}) %collective-permute-start.18) | collective-permute-done | bytes 524320 | tf_op jit(solution)/shard_map/ppermute | solution.py:388
  123.8 7.6 %collective-permute-done.28.refs_24_ = bf16[1024,256]{1,0:T(8,128)(2,1)} collective-permute-done((bf16[1024,256]{1,0:T(8,128)(2,1)}, bf16[1024,256]{1,0:T(8,128)(2,1)}, u32[]{:S(2)}, u32[]{:S(2)}) %collective-permute-start.28) | collective-permute-done | bytes 524320 | tf_op jit(solution)/shard_map/ppermute | solution.py:388
  133.6 9.1 %collective-permute-done.19.refs_23_ = bf16[1024,256]{1,0:T(8,128)(2,1)} collective-permute-done((bf16[1024,256]{1,0:T(8,128)(2,1)}, bf16[1024,256]{1,0:T(8,128)(2,1)}, u32[]{:S(2)}, u32[]{:S(2)}) %collective-permute-start.19) | collective-permute-done | bytes 524320 | tf_op jit(solution)/shard_map/ppermute | solution.py:388
  153.8 17.0 %couple_early.1.refs_5_ = f32[4096,256]{1,0:T(8,128)S(1)} custom-call(s32[8,8]{1,0:T(8,128)S(1)} %get-tuple-element.39.origin_ref, s32[8,8]{1,0:T(8,128)S(1)} %get-tuple-element.38.offset_ref, s32[8]{0:T(128)S(1)} %broadcast_in_dim.58.first_ref, s32[8]{0:T(128)S(1)} %sub.84.count_ref.first_ref, s32[8,8]{1,0:T(8,128)S(1)} %get-tuple-element.37.kind_ref, ...), custom_call_target="tpu_custom_call" | custom-call | flops 4294967296 | bytes 16777216 | tf_op jit(solution)/shard_map/couple_early/pallas_call | solution.py:149
  170.8 6.0 %couple_late.1 = (bf16[4096,256]{1,0:T(8,128)(2,1)S(1)}, f32[256,512]{1,0:T(8,128)S(1)}) custom-call(s32[8,8]{1,0:T(8,128)S(1)} %get-tuple-element.39.origin_ref, s32[8,8]{1,0:T(8,128)S(1)} %get-tuple-element.38.offset_ref, s32[8]{0:T(128)S(1)} %sub.84.count_ref.first_ref, s32[8]{0:T(128)S(1)} %get-tuple-element.40.count_ref, ...), custom_call_target="tpu_custom_call" | custom-call | tf_op jit(solution)/shard_map/couple_late/pallas_call | solution.py:182
  180.0 5.6 %collective-permute-done.31 = f32[64,512]{1,0:T(8,128)S(1)} collective-permute-done((f32[64,512]{1,0:T(8,128)S(1)}, f32[64,512]{1,0:T(8,128)S(1)}, u32[]{:S(2)}, u32[]{:S(2)}) %collective-permute-start.31) | collective-permute-done | bytes 131104 | tf_op jit(solution)/shard_map/ppermute | solution.py:430
  187.0 3.4 %collective-permute-done.32 = f32[32,768]{1,0:T(8,128)S(1)} collective-permute-done((f32[32,768]{1,0:T(8,128)S(1)}, f32[32,768]{1,0:T(8,128)S(1)}, u32[]{:S(2)}, u32[]{:S(2)}) %collective-permute-start.32) | collective-permute-done | bytes 98336 | tf_op jit(solution)/shard_map/ppermute | solution.py:430
  190.4 4.2 %collective-permute-start.33 = (f32[32,768]{1,0:T(8,128)S(1)}, f32[32,768]{1,0:T(8,128)S(1)}, u32[]{:S(2)}, u32[]{:S(2)}) collective-permute-start(f32[32,768]{1,0:T(8,128)S(1)} %fusion.2), channel_id=1, source_target_pairs={{0,2},{1,3},{2,0},{3,1},{4,6},{5,7},{6,4},{7,5},{8,10},{9,11},{10,... | collective-permute-start | bytes 294920 | tf_op jit(solution)/shard_map/ppermute | solution.py:430
  194.6 2.6 %collective-permute-done.33 = f32[32,768]{1,0:T(8,128)S(1)} collective-permute-done((f32[32,768]{1,0:T(8,128)S(1)}, f32[32,768]{1,0:T(8,128)S(1)}, u32[]{:S(2)}, u32[]{:S(2)}) %collective-permute-start.33) | collective-permute-done | bytes 98336 | tf_op jit(solution)/shard_map/ppermute | solution.py:430
  197.2 5.5 %collective-permute-start.34 = (f32[32,768]{1,0:T(8,128)S(1)}, f32[32,768]{1,0:T(8,128)S(1)}, u32[]{:S(2)}, u32[]{:S(2)}) collective-permute-start(f32[32,768]{1,0:T(8,128)S(1)} %add.183), channel_id=1, source_target_pairs={{0,4},{1,5},{2,6},{3,7},{4,0},{5,1},{6,2},{7,3},{8,12},{9,13},{10,... | collective-permute-start | bytes 294920 | tf_op jit(solution)/shard_map/ppermute | solution.py:430
  202.8 2.6 %collective-permute-done.34 = f32[32,768]{1,0:T(8,128)S(1)} collective-permute-done((f32[32,768]{1,0:T(8,128)S(1)}, f32[32,768]{1,0:T(8,128)S(1)}, u32[]{:S(2)}, u32[]{:S(2)}) %collective-permute-start.34) | collective-permute-done | bytes 98336 | tf_op jit(solution)/shard_map/ppermute | solution.py:430
  207.3 2.8 %collective-permute-done.35 = f32[32,768]{1,0:T(8,128)S(1)} collective-permute-done((f32[32,768]{1,0:T(8,128)S(1)}, f32[32,768]{1,0:T(8,128)S(1)}, u32[]{:S(2)}, u32[]{:S(2)}) %collective-permute-start.35) | collective-permute-done | bytes 98336 | tf_op jit(solution)/shard_map/ppermute | solution.py:430
  210.8 5.1 %collective-permute-done.36 = f32[64,768]{1,0:T(8,128)S(1)} collective-permute-done((f32[64,768]{1,0:T(8,128)S(1)}, f32[64,768]{1,0:T(8,128)S(1)}, u32[]{:S(2)}, u32[]{:S(2)}) %collective-permute-start.36) | collective-permute-done | bytes 196640 | tf_op jit(solution)/shard_map/ppermute | solution.py:430
  219.3 24.5 %finish.1 = bf16[4096,256]{1,0:T(8,128)(2,1)} custom-call(s32[8]{0:T(128)S(1)} %stack.35.order_ref, f32[256,768]{1,0:T(8,128)S(1)} %pad_maximum_fusion.chunks_ref, bf16[4096,256]{1,0:T(8,128)(2,1)S(1)} %copy-done.7, bf16[4096,256]{1,0:T(8,128)(2,1)S(1)} %copy-done.3), custom_call_target="tpu_custom_call" | custom-call | tf_op jit(solution)/shard_map/finish/pallas_call | solution.py:331
  (127 shorter events, 47.7 us)
Async XLA Ops:
  3.0 15.9 %collective-permute-start.21 = (bf16[1024,256]{1,0:T(8,128)(2,1)}, bf16[1024,256]{1,0:T(8,128)(2,1)S(1)}, u32[]{:S(2)}, u32[]{:S(2)}) collective-permute-start(bf16[1024,256]{1,0:T(8,128)(2,1)} %get-tuple-element.42), channel_id=1, source_target_pairs={{1,0},{3,1},{5,3},{7,5},{6,7},{4,6},{2,4},{0,2},{9,8},{11,9},{13,1... | collective-permute-start | bytes 1572872 | tf_op jit(solution)/shard_map/ppermute | solution.py:388
  6.0 15.2 %collective-permute-start.7 = (bf16[1024,256]{1,0:T(8,128)(2,1)}, bf16[1024,256]{1,0:T(8,128)(2,1)S(1)}, u32[]{:S(2)}, u32[]{:S(2)}) collective-permute-start(bf16[1024,256]{1,0:T(8,128)(2,1)} %get-tuple-element.44), channel_id=1, source_target_pairs={{0,1},{1,3},{3,5},{5,7},{7,6},{6,4},{4,2},{2,0},{8,9},{9,11},{11,1... | collective-permute-start | bytes 1572872 | tf_op jit(solution)/shard_map/ppermute | solution.py:388
  6.0 24.2 %collective-permute-start.14 = (bf16[1024,256]{1,0:T(8,128)(2,1)}, bf16[1024,256]{1,0:T(8,128)(2,1)}, u32[]{:S(2)}, u32[]{:S(2)}) collective-permute-start(bf16[1024,256]{1,0:T(8,128)(2,1)} %get-tuple-element.43), channel_id=1, source_target_pairs={{1,0},{3,1},{5,3},{7,5},{6,7},{4,6},{2,4},{0,2},{9,8},{11,9},{13,1... | collective-permute-start | bytes 1572872 | tf_op jit(solution)/shard_map/ppermute | solution.py:388
  8.1 24.4 %collective-permute-start = (bf16[1024,256]{1,0:T(8,128)(2,1)}, bf16[1024,256]{1,0:T(8,128)(2,1)}, u32[]{:S(2)}, u32[]{:S(2)}) collective-permute-start(bf16[1024,256]{1,0:T(8,128)(2,1)} %get-tuple-element.45), channel_id=1, source_target_pairs={{0,1},{1,3},{3,5},{5,7},{7,6},{6,4},{4,2},{2,0},{8,9},{9,11},{11,1... | collective-permute-start | bytes 1572872 | tf_op jit(solution)/shard_map/ppermute | solution.py:388
  18.9 13.5 %collective-permute-start.23 = (f32[128,256]{1,0:T(8,128)S(1)}, f32[128,256]{1,0:T(8,128)}, u32[]{:S(2)}, u32[]{:S(2)}) collective-permute-start(f32[128,256]{1,0:T(8,128)S(1)} %constant_dynamic-slice_fusion.3), channel_id=1, source_target_pairs={{0,8},{8,0},{16,24},{24,16},{1,9},{9,1},{17,25},{25,17},{2,10},{10... | collective-permute-start | bytes 393224 | tf_op jit(solution)/shard_map/ppermute | solution.py:430
  19.1 22.4 %collective-permute-start.22 = (bf16[1024,256]{1,0:T(8,128)(2,1)S(1)}, bf16[1024,256]{1,0:T(8,128)(2,1)}, u32[]{:S(2)}, u32[]{:S(2)}) collective-permute-start(bf16[1024,256]{1,0:T(8,128)(2,1)S(1)} %collective-permute-done.21.refs_4_), channel_id=1, source_target_pairs={{1,0},{3,1},{5,3},{7,5},{6,7},{4,6},{2,4},{0,2},{9,8},{11,9},{13,1... | collective-permute-start | bytes 1572872 | tf_op jit(solution)/shard_map/ppermute | solution.py:388
  21.2 22.4 %collective-permute-start.8 = (bf16[1024,256]{1,0:T(8,128)(2,1)S(1)}, bf16[1024,256]{1,0:T(8,128)(2,1)}, u32[]{:S(2)}, u32[]{:S(2)}) collective-permute-start(bf16[1024,256]{1,0:T(8,128)(2,1)S(1)} %collective-permute-done.7.refs_2_), channel_id=1, source_target_pairs={{0,1},{1,3},{3,5},{5,7},{7,6},{6,4},{4,2},{2,0},{8,9},{9,11},{11,1... | collective-permute-start | bytes 1572872 | tf_op jit(solution)/shard_map/ppermute | solution.py:388
  30.3 22.5 %collective-permute-start.15 = (bf16[1024,256]{1,0:T(8,128)(2,1)}, bf16[1024,256]{1,0:T(8,128)(2,1)}, u32[]{:S(2)}, u32[]{:S(2)}) collective-permute-start(bf16[1024,256]{1,0:T(8,128)(2,1)} %collective-permute-done.14.refs_3_), channel_id=1, source_target_pairs={{1,0},{3,1},{5,3},{7,5},{6,7},{4,6},{2,4},{0,2},{9,8},{11,9},{13,1... | collective-permute-start | bytes 1572872 | tf_op jit(solution)/shard_map/ppermute | solution.py:388
  32.4 22.5 %collective-permute-start.1 = (bf16[1024,256]{1,0:T(8,128)(2,1)}, bf16[1024,256]{1,0:T(8,128)(2,1)}, u32[]{:S(2)}, u32[]{:S(2)}) collective-permute-start(bf16[1024,256]{1,0:T(8,128)(2,1)} %collective-permute-done.refs_1_), channel_id=1, source_target_pairs={{0,1},{1,3},{3,5},{5,7},{7,6},{6,4},{4,2},{2,0},{8,9},{9,11},{11,1... | collective-permute-start | bytes 1572872 | tf_op jit(solution)/shard_map/ppermute | solution.py:388
  41.5 22.4 %collective-permute-start.25 = (bf16[1024,256]{1,0:T(8,128)(2,1)}, bf16[1024,256]{1,0:T(8,128)(2,1)S(1)}, u32[]{:S(2)}, u32[]{:S(2)}) collective-permute-start(bf16[1024,256]{1,0:T(8,128)(2,1)} %collective-permute-done.22.refs_8_), channel_id=1, source_target_pairs={{1,0},{3,1},{5,3},{7,5},{6,7},{4,6},{2,4},{0,2},{9,8},{11,9},{13,1... | collective-permute-start | bytes 1572872 | tf_op jit(solution)/shard_map/ppermute | solution.py:388
  43.7 23.1 %collective-permute-start.9 = (bf16[1024,256]{1,0:T(8,128)(2,1)}, bf16[1024,256]{1,0:T(8,128)(2,1)S(1)}, u32[]{:S(2)}, u32[]{:S(2)}) collective-permute-start(bf16[1024,256]{1,0:T(8,128)(2,1)} %collective-permute-done.8.refs_6_), channel_id=1, source_target_pairs={{0,1},{1,3},{3,5},{5,7},{7,6},{6,4},{4,2},{2,0},{8,9},{9,11},{11,1... | collective-permute-start | bytes 1572872 | tf_op jit(solution)/shard_map/ppermute | solution.py:388
  52.7 22.4 %collective-permute-start.16 = (bf16[1024,256]{1,0:T(8,128)(2,1)}, bf16[1024,256]{1,0:T(8,128)(2,1)S(1)}, u32[]{:S(2)}, u32[]{:S(2)}) collective-permute-start(bf16[1024,256]{1,0:T(8,128)(2,1)} %collective-permute-done.15.refs_7_), channel_id=1, source_target_pairs={{1,0},{3,1},{5,3},{7,5},{6,7},{4,6},{2,4},{0,2},{9,8},{11,9},{13,1... | collective-permute-start | bytes 1572872 | tf_op jit(solution)/shard_map/ppermute | solution.py:388
  54.9 23.1 %collective-permute-start.2 = (bf16[1024,256]{1,0:T(8,128)(2,1)}, bf16[1024,256]{1,0:T(8,128)(2,1)S(1)}, u32[]{:S(2)}, u32[]{:S(2)}) collective-permute-start(bf16[1024,256]{1,0:T(8,128)(2,1)} %collective-permute-done.1.refs_5_), channel_id=1, source_target_pairs={{0,1},{1,3},{3,5},{5,7},{7,6},{6,4},{4,2},{2,0},{8,9},{9,11},{11,1... | collective-permute-start | bytes 1572872 | tf_op jit(solution)/shard_map/ppermute | solution.py:388
  63.9 22.6 %collective-permute-start.26 = (bf16[1024,256]{1,0:T(8,128)(2,1)S(1)}, bf16[1024,256]{1,0:T(8,128)(2,1)}, u32[]{:S(2)}, u32[]{:S(2)}) collective-permute-start(bf16[1024,256]{1,0:T(8,128)(2,1)S(1)} %collective-permute-done.25.refs_12_), channel_id=1, source_target_pairs={{1,0},{3,1},{5,3},{7,5},{6,7},{4,6},{2,4},{0,2},{9,8},{11,9},{13,1... | collective-permute-start | bytes 1572872 | tf_op jit(solution)/shard_map/ppermute | solution.py:388
  66.8 21.8 %collective-permute-start.10 = (bf16[1024,256]{1,0:T(8,128)(2,1)S(1)}, bf16[1024,256]{1,0:T(8,128)(2,1)}, u32[]{:S(2)}, u32[]{:S(2)}) collective-permute-start(bf16[1024,256]{1,0:T(8,128)(2,1)S(1)} %collective-permute-done.9.refs_10_), channel_id=1, source_target_pairs={{0,1},{1,3},{3,5},{5,7},{7,6},{6,4},{4,2},{2,0},{8,9},{9,11},{11,1... | collective-permute-start | bytes 1572872 | tf_op jit(solution)/shard_map/ppermute | solution.py:388
  75.1 22.6 %collective-permute-start.17 = (bf16[1024,256]{1,0:T(8,128)(2,1)S(1)}, bf16[1024,256]{1,0:T(8,128)(2,1)}, u32[]{:S(2)}, u32[]{:S(2)}) collective-permute-start(bf16[1024,256]{1,0:T(8,128)(2,1)S(1)} %collective-permute-done.16.refs_11_), channel_id=1, source_target_pairs={{1,0},{3,1},{5,3},{7,5},{6,7},{4,6},{2,4},{0,2},{9,8},{11,9},{13,1... | collective-permute-start | bytes 1572872 | tf_op jit(solution)/shard_map/ppermute | solution.py:388
  78.0 21.8 %collective-permute-start.3 = (bf16[1024,256]{1,0:T(8,128)(2,1)S(1)}, bf16[1024,256]{1,0:T(8,128)(2,1)}, u32[]{:S(2)}, u32[]{:S(2)}) collective-permute-start(bf16[1024,256]{1,0:T(8,128)(2,1)S(1)} %collective-permute-done.2.refs_9_), channel_id=1, source_target_pairs={{0,1},{1,3},{3,5},{5,7},{7,6},{6,4},{4,2},{2,0},{8,9},{9,11},{11,1... | collective-permute-start | bytes 1572872 | tf_op jit(solution)/shard_map/ppermute | solution.py:388
  86.5 22.5 %collective-permute-start.27 = (bf16[1024,256]{1,0:T(8,128)(2,1)}, bf16[1024,256]{1,0:T(8,128)(2,1)}, u32[]{:S(2)}, u32[]{:S(2)}) collective-permute-start(bf16[1024,256]{1,0:T(8,128)(2,1)} %collective-permute-done.26.refs_16_), channel_id=1, source_target_pairs={{1,0},{3,1},{5,3},{7,5},{6,7},{4,6},{2,4},{0,2},{9,8},{11,9},{13,1... | collective-permute-start | bytes 1572872 | tf_op jit(solution)/shard_map/ppermute | solution.py:388
  88.6 22.5 %collective-permute-start.11 = (bf16[1024,256]{1,0:T(8,128)(2,1)}, bf16[1024,256]{1,0:T(8,128)(2,1)}, u32[]{:S(2)}, u32[]{:S(2)}) collective-permute-start(bf16[1024,256]{1,0:T(8,128)(2,1)} %collective-permute-done.10.refs_14_), channel_id=1, source_target_pairs={{0,1},{1,3},{3,5},{5,7},{7,6},{6,4},{4,2},{2,0},{8,9},{9,11},{11,1... | collective-permute-start | bytes 1572872 | tf_op jit(solution)/shard_map/ppermute | solution.py:388
  97.7 22.5 %collective-permute-start.18 = (bf16[1024,256]{1,0:T(8,128)(2,1)}, bf16[1024,256]{1,0:T(8,128)(2,1)}, u32[]{:S(2)}, u32[]{:S(2)}) collective-permute-start(bf16[1024,256]{1,0:T(8,128)(2,1)} %collective-permute-done.17.refs_15_), channel_id=1, source_target_pairs={{1,0},{3,1},{5,3},{7,5},{6,7},{4,6},{2,4},{0,2},{9,8},{11,9},{13,1... | collective-permute-start | bytes 1572872 | tf_op jit(solution)/shard_map/ppermute | solution.py:388
  99.8 22.5 %collective-permute-start.4 = (bf16[1024,256]{1,0:T(8,128)(2,1)}, bf16[1024,256]{1,0:T(8,128)(2,1)}, u32[]{:S(2)}, u32[]{:S(2)}) collective-permute-start(bf16[1024,256]{1,0:T(8,128)(2,1)} %collective-permute-done.3.refs_13_), channel_id=1, source_target_pairs={{0,1},{1,3},{3,5},{5,7},{7,6},{6,4},{4,2},{2,0},{8,9},{9,11},{11,1... | collective-permute-start | bytes 1572872 | tf_op jit(solution)/shard_map/ppermute | solution.py:388
  108.9 22.5 %collective-permute-start.28 = (bf16[1024,256]{1,0:T(8,128)(2,1)}, bf16[1024,256]{1,0:T(8,128)(2,1)}, u32[]{:S(2)}, u32[]{:S(2)}) collective-permute-start(bf16[1024,256]{1,0:T(8,128)(2,1)} %collective-permute-done.27.refs_20_), channel_id=1, source_target_pairs={{1,0},{3,1},{5,3},{7,5},{6,7},{4,6},{2,4},{0,2},{9,8},{11,9},{13,1... | collective-permute-start | bytes 1572872 | tf_op jit(solution)/shard_map/ppermute | solution.py:388
  111.1 22.5 %collective-permute-start.12 = (bf16[1024,256]{1,0:T(8,128)(2,1)}, bf16[1024,256]{1,0:T(8,128)(2,1)}, u32[]{:S(2)}, u32[]{:S(2)}) collective-permute-start(bf16[1024,256]{1,0:T(8,128)(2,1)} %collective-permute-done.11.refs_18_), channel_id=1, source_target_pairs={{0,1},{1,3},{3,5},{5,7},{7,6},{6,4},{4,2},{2,0},{8,9},{9,11},{11,1... | collective-permute-start | bytes 1572872 | tf_op jit(solution)/shard_map/ppermute | solution.py:388
  120.2 22.5 %collective-permute-start.19 = (bf16[1024,256]{1,0:T(8,128)(2,1)}, bf16[1024,256]{1,0:T(8,128)(2,1)}, u32[]{:S(2)}, u32[]{:S(2)}) collective-permute-start(bf16[1024,256]{1,0:T(8,128)(2,1)} %collective-permute-done.18.refs_19_), channel_id=1, source_target_pairs={{1,0},{3,1},{5,3},{7,5},{6,7},{4,6},{2,4},{0,2},{9,8},{11,9},{13,1... | collective-permute-start | bytes 1572872 | tf_op jit(solution)/shard_map/ppermute | solution.py:388
  122.3 22.5 %collective-permute-start.5 = (bf16[1024,256]{1,0:T(8,128)(2,1)}, bf16[1024,256]{1,0:T(8,128)(2,1)}, u32[]{:S(2)}, u32[]{:S(2)}) collective-permute-start(bf16[1024,256]{1,0:T(8,128)(2,1)} %collective-permute-done.4.refs_17_), channel_id=1, source_target_pairs={{0,1},{1,3},{3,5},{5,7},{7,6},{6,4},{4,2},{2,0},{8,9},{9,11},{11,1... | collective-permute-start | bytes 1572872 | tf_op jit(solution)/shard_map/ppermute | solution.py:388
  131.4 39.4 %collective-permute-start.29 = (bf16[1024,256]{1,0:T(8,128)(2,1)}, bf16[1024,256]{1,0:T(8,128)(2,1)S(1)}, u32[]{:S(2)}, u32[]{:S(2)}) collective-permute-start(bf16[1024,256]{1,0:T(8,128)(2,1)} %collective-permute-done.28.refs_24_), channel_id=1, source_target_pairs={{1,0},{3,1},{5,3},{7,5},{6,7},{4,6},{2,4},{0,2},{9,8},{11,9},{13,1... | collective-permute-start | bytes 1572872 | tf_op jit(solution)/shard_map/ppermute | solution.py:388
  133.6 37.2 %collective-permute-start.13 = (bf16[1024,256]{1,0:T(8,128)(2,1)}, bf16[1024,256]{1,0:T(8,128)(2,1)S(1)}, u32[]{:S(2)}, u32[]{:S(2)}) collective-permute-start(bf16[1024,256]{1,0:T(8,128)(2,1)} %collective-permute-done.12.refs_22_), channel_id=1, source_target_pairs={{0,1},{1,3},{3,5},{5,7},{7,6},{6,4},{4,2},{2,0},{8,9},{9,11},{11,1... | collective-permute-start | bytes 1572872 | tf_op jit(solution)/shard_map/ppermute | solution.py:388
  142.6 28.2 %collective-permute-start.20 = (bf16[1024,256]{1,0:T(8,128)(2,1)}, bf16[1024,256]{1,0:T(8,128)(2,1)}, u32[]{:S(2)}, u32[]{:S(2)}) collective-permute-start(bf16[1024,256]{1,0:T(8,128)(2,1)} %collective-permute-done.19.refs_23_), channel_id=1, source_target_pairs={{1,0},{3,1},{5,3},{7,5},{6,7},{4,6},{2,4},{0,2},{9,8},{11,9},{13,1... | collective-permute-start | bytes 1572872 | tf_op jit(solution)/shard_map/ppermute | solution.py:388
  144.8 26.0 %collective-permute-start.6 = (bf16[1024,256]{1,0:T(8,128)(2,1)}, bf16[1024,256]{1,0:T(8,128)(2,1)}, u32[]{:S(2)}, u32[]{:S(2)}) collective-permute-start(bf16[1024,256]{1,0:T(8,128)(2,1)} %collective-permute-done.5.refs_21_), channel_id=1, source_target_pairs={{0,1},{1,3},{3,5},{5,7},{7,6},{6,4},{4,2},{2,0},{8,9},{9,11},{11,1... | collective-permute-start | bytes 1572872 | tf_op jit(solution)/shard_map/ppermute | solution.py:388
  179.9 5.7 %collective-permute-start.31 = (f32[64,512]{1,0:T(8,128)S(1)}, f32[64,512]{1,0:T(8,128)S(1)}, u32[]{:S(2)}, u32[]{:S(2)}) collective-permute-start(f32[64,512]{1,0:T(8,128)S(1)} %constant_dynamic-slice_fusion), channel_id=1, source_target_pairs={{0,16},{8,24},{16,0},{24,8},{1,17},{9,25},{17,1},{25,9},{2,18},{10... | collective-permute-start | bytes 393224 | tf_op jit(solution)/shard_map/ppermute | solution.py:430
  190.4 6.8 %collective-permute-start.33 = (f32[32,768]{1,0:T(8,128)S(1)}, f32[32,768]{1,0:T(8,128)S(1)}, u32[]{:S(2)}, u32[]{:S(2)}) collective-permute-start(f32[32,768]{1,0:T(8,128)S(1)} %fusion.2), channel_id=1, source_target_pairs={{0,2},{1,3},{2,0},{3,1},{4,6},{5,7},{6,4},{7,5},{8,10},{9,11},{10,... | collective-permute-start | bytes 294920 | tf_op jit(solution)/shard_map/ppermute | solution.py:430
  197.2 8.1 %collective-permute-start.34 = (f32[32,768]{1,0:T(8,128)S(1)}, f32[32,768]{1,0:T(8,128)S(1)}, u32[]{:S(2)}, u32[]{:S(2)}) collective-permute-start(f32[32,768]{1,0:T(8,128)S(1)} %add.183), channel_id=1, source_target_pairs={{0,4},{1,5},{2,6},{3,7},{4,0},{5,1},{6,2},{7,3},{8,12},{9,13},{10,... | collective-permute-start | bytes 294920 | tf_op jit(solution)/shard_map/ppermute | solution.py:430
  (32 other events, 769.0 us)
where the time goes:
time: 244 us
  waiting for transfers between devices  120 us (49%)
  Pallas kernels  53 us (22%)
  starting transfers between devices  46.8 us (19%)
  local copies, waits for them, and re-layouts  20.8 us (9%)
  other arithmetic  3.33 us (1%)
    ppermute x28, waiting for transfers between devices, ring_gather(): lax.ppermute(piece, 'col', forward if i < PIECES // 2 else back)  92.3 us
    ppermute x28, starting transfers between devices, ring_gather(): lax.ppermute(piece, 'col', forward if i < PIECES // 2 else back)  30.6 us
    ppermute x10, waiting for transfers between devices, swap(): return lax.ppermute(value, axis, [(i, i ^ stride) for i in range(count)])  27.3 us
    pallas_call x1, Pallas kernels, finish_part(): pl.pallas_call(finish_kernel, in_specs=[pl.BlockSpec(memory_space=pltpu.S...  24.5 us
    pallas_call x1, Pallas kernels, early_part(): pl.pallas_call(early_kernel, grid_spec=pltpu.PrefetchScalarGridSpec(num_s...  17 us
    unnamed x52, local copies, waits for them, and re-layouts  16.9 us
    ppermute x10, starting transfers between devices, swap(): return lax.ppermute(value, axis, [(i, i ^ stride) for i in range(count)])  16.2 us
    pallas_call x1, Pallas kernels, late_part(): pl.pallas_call(late_kernel, grid_spec=pltpu.PrefetchScalarGridSpec(num_sc...  6.05 us
  transfers between devices with their start and end apart: 38, of which 21 were waited for; matrix products, arithmetic and copies ran while one was open for 2% of the time, Pallas kernels for 9%

commit v1 on v0

--- a/solution.py
+++ b/solution.py
@@ -47,7 +47,7 @@
             jax.ShapeDtypeStruct((rows, rank), jnp.bfloat16),
             jax.ShapeDtypeStruct((rank, rank), jnp.float32),
         ],
-        compiler_params=pltpu.CompilerParams(vmem_limit_bytes=12 * 2**20),
+        compiler_params=pltpu.CompilerParams(vmem_limit_bytes=7 * 2**20),
         name="bath",
     )(bath_pattern, bath_blocks, own)
 
@@ -105,15 +105,26 @@
 
 
 def early_kernel(origin_ref, offset_ref, first_ref, count_ref, kind_ref, *refs):
-    sources = refs[:-6]
-    coupling_ref, own_ref, energy_ref, total_ref, held, sems = refs[-6:]
+    sources = refs[:-8]
+    coupling_hbm, own_ref, energy_ref, total_ref, coupling, held, sems, coupling_sem = refs[-8:]
     block_rows = own_ref.shape[0]
+    load = pltpu.make_async_copy(coupling_hbm, coupling, coupling_sem)
+
+    @pl.when(pl.program_id(0) == 0)
+    def _():
+        load.start()
+
     row = energy_ref[pl.ds(pl.program_id(0), 1), :]
     energy = jnp.broadcast_to(row, (8, block_rows)).T[:, :1]
     wide = own_ref[...].astype(jnp.float32)
     total_ref[...] = wide - time_step * (energy * wide)
+
+    @pl.when(pl.program_id(0) == 0)
+    def _():
+        load.wait()
+
     gather_products(
-        origin_ref, offset_ref, first_ref, count_ref, kind_ref, sources, coupling_ref, held, sems, total_ref
+        origin_ref, offset_ref, first_ref, count_ref, kind_ref, sources, coupling, held, sems, total_ref
     )
 
 
@@ -152,19 +163,21 @@
             num_scalar_prefetch=5,
             grid=(blocks,),
             in_specs=[
-                *[pl.BlockSpec(memory_space=pl.ANY) for _ in sources],
-                pl.BlockSpec((kinds, block_rows, block_rows), lambda b, *_: (0, 0, 0)),
+                *[pl.BlockSpec(memory_space=pltpu.HBM) for _ in sources],
+                pl.BlockSpec(memory_space=pltpu.HBM),
                 tile,
                 pl.BlockSpec((blocks, block_rows), lambda b, *_: (0, 0)),
             ],
             out_specs=tile,
             scratch_shapes=[
+                pltpu.VMEM((kinds, block_rows, block_rows), jnp.bfloat16),
                 pltpu.VMEM((2, slots, block_rows, rank), jnp.bfloat16),
                 pltpu.SemaphoreType.DMA((2, slots)),
+                pltpu.SemaphoreType.DMA,
             ],
         ),
         out_shape=jax.ShapeDtypeStruct((rows, rank), jnp.float32),
-        compiler_params=pltpu.CompilerParams(vmem_limit_bytes=16 * 2**20),
+        compiler_params=pltpu.CompilerParams(vmem_limit_bytes=10 * 2**20),
         cost_estimate=pl.CostEstimate(
             flops=blocks * slots * block_rows * block_rows * rank,
             bytes_accessed=blocks * slots * block_rows * rank * 2,
@@ -201,7 +214,7 @@
             jax.ShapeDtypeStruct((rows, rank), jnp.bfloat16),
             jax.ShapeDtypeStruct((rank, 2 * rank), jnp.float32),
         ],
-        compiler_params=pltpu.CompilerParams(vmem_limit_bytes=20 * 2**20),
+        compiler_params=pltpu.CompilerParams(vmem_limit_bytes=14 * 2**20),
         name="couple_late",
     )(*lists, *sources, coupling_blocks, base, bathed)
 
@@ -214,27 +227,32 @@
     work = jnp.concatenate([square, eye], axis=1)
     bands = [work[8 * i : 8 * i + 8, :] for i in range(n // 8)]
     sublane = lax.broadcasted_iota(jnp.int32, (8, 2 * n), 0)
+    def spread(band, g):
+        return [jnp.broadcast_to(band[:, 8 * g + r : 8 * g + r + 1], (8, 2 * n)) for r in range(8)]
+
     out = []
     for g in range(n // 8):
-        below = range(g, n // 8)
-        columns = {
-            i: [jnp.broadcast_to(bands[i][:, 8 * g + r : 8 * g + r + 1], (8, 2 * n)) for r in range(8)]
-            for i in below
-        }
+        band = bands[g]
+        pivots = spread(band, g)
         diagonal = jnp.zeros((8, 2 * n), jnp.float32)
+        scales = []
         for r in range(8):
-            pivots = [columns[g][q][r : r + 1, :] for q in range(r, 8)]
-            scale = pl.reciprocal(pivots[0], approx=True)
-            diagonal = jnp.where(sublane == r, columns[g][r], diagonal)
-            row = bands[g][r : r + 1, :]
-            for i in below:
-                share = columns[i][r] * scale
-                if i == g:
-                    share = jnp.where(sublane > r, share, 0.0)
+            scales.append(pl.reciprocal(pivots[r][r : r + 1, :], approx=True))
+            diagonal = jnp.where(sublane == r, pivots[r], diagonal)
+            share = jnp.where(sublane > r, pivots[r] * scales[r], 0.0)
+            for q in range(r + 1, 8):
+                pivots[q] = pivots[q] - share * pivots[q][r : r + 1, :]
+            band = band - share * band[r : r + 1, :]
+        out.append(band[:, n:] * lax.rsqrt(diagonal)[:, n:])
+        for i in range(g + 1, n // 8):
+            columns = spread(bands[i], g)
+            below = bands[i]
+            for r in range(8):
+                share = columns[r] * scales[r]
                 for q in range(r + 1, 8):
-                    columns[i][q] = columns[i][q] - share * pivots[q - r]
-                bands[i] = bands[i] - share * row
-        out.append(bands[g][:, n:] * lax.rsqrt(diagonal)[:, n:])
+                    columns[q] = columns[q] - share * pivots[q][r : r + 1, :]
+                below = below - share * band[r : r + 1, :]
+            bands[i] = below
     return jnp.concatenate(out, axis=0)
 
 
@@ -293,7 +311,7 @@
             precision=HIGHEST, preferred_element_type=jnp.float32,
         )
     eliminate(inner, image)
-    rotation = image[...].astype(jnp.bfloat16)
+    rotation = image[...].T.astype(jnp.bfloat16)
     load_moved.wait()
     load_bathed.wait()
     pieces = out_sems.shape[0]
@@ -305,14 +323,8 @@
 
     def one(piece, carry):
         rows = pl.ds(pl.multiple_of(piece * size, size), size)
-        value = lax.dot_general(
-            moved[rows, :], rotation[:, :rank], (((1,), (1,)), ((), ())),
-            preferred_element_type=jnp.float32,
-        )
-        value += lax.dot_general(
-            bathed[rows, :], rotation[:, rank:], (((1,), (1,)), ((), ())),
-            preferred_element_type=jnp.float32,
-        )
+        stacked = jnp.concatenate([moved[rows, :], bathed[rows, :]], axis=1)
+        value = jnp.dot(stacked, rotation, preferred_element_type=jnp.float32)
         out[rows, :] = value.astype(jnp.bfloat16)
         store(piece).start()
         return carry
@@ -333,8 +345,8 @@
         in_specs=[
             pl.BlockSpec(memory_space=pltpu.SMEM),
             pl.BlockSpec(memory_space=pltpu.VMEM),
-            pl.BlockSpec(memory_space=pl.ANY),
-            pl.BlockSpec(memory_space=pl.ANY),
+            pl.BlockSpec(memory_space=pltpu.HBM),
+            pl.BlockSpec(memory_space=pltpu.HBM),
         ],
         out_specs=pl.BlockSpec(memory_space=pl.ANY),
         out_shape=jax.ShapeDtypeStruct((rows, rank), jnp.bfloat16),
@@ -348,7 +360,7 @@
             pltpu.SemaphoreType.DMA((2,)),
             pltpu.SemaphoreType.DMA((8,)),
         ],
-        compiler_params=pltpu.CompilerParams(vmem_limit_bytes=24 * 2**20),
+        compiler_params=pltpu.CompilerParams(vmem_limit_bytes=14 * 2**20),
         name="finish",
     )(order, chunks, moved, bathed)
 

time: 244 us -> 245 us (level)
  Pallas kernels: 53 us -> 49.6 us
  starting transfers between devices: 46.8 us -> 49.5 us
    pallas_call x1, Pallas kernels: 17 us -> 12.9 us  [early_part(): pl.pallas_call(early_kernel, grid_spec=pltpu.PrefetchScalarGridSpec(num_s...]
    ppermute x10, starting transfers between devices: 16.2 us -> 18.9 us  [swap(): return lax.ppermute(value, axis, [(i, i ^ stride) for i in range(count)])]
  transfers between devices with their start and end apart: 38 -> 38, of which waited for: 21 -> 21; matrix products, arithmetic and copies ran while one was open for 2% -> 2% of each run, Pallas kernels for 9% -> 8%
where the time goes in v1:
time: 245 us; the launch traced here: 244 us
  waiting for transfers between devices  120 us (49%)
  Pallas kernels  49.6 us (20%)
  starting transfers between devices  49.5 us (20%)
  local copies, waits for them, and re-layouts  20.8 us (8%)
  other arithmetic  3.33 us (1%)
    ppermute x28, waiting for transfers between devices, ring_gather(): lax.ppermute(piece, 'col', forward if i < PIECES // 2 else back)  92.3 us
    ppermute x28, starting transfers between devices, ring_gather(): lax.ppermute(piece, 'col', forward if i < PIECES // 2 else back)  30.6 us
    ppermute x10, waiting for transfers between devices, swap(): return lax.ppermute(value, axis, [(i, i ^ stride) for i in range(count)])  27.7 us
    pallas_call x1, Pallas kernels, finish_part(): pl.pallas_call(finish_kernel, in_specs=[pl.BlockSpec(memory_space=pltpu.S...  24.6 us
    ppermute x10, starting transfers between devices, swap(): return lax.ppermute(value, axis, [(i, i ^ stride) for i in range(count)])  18.9 us
    unnamed x52, local copies, waits for them, and re-layouts  16.9 us
    pallas_call x1, Pallas kernels, early_part(): pl.pallas_call(early_kernel, grid_spec=pltpu.PrefetchScalarGridSpec(num_s...  12.9 us
    pallas_call x1, Pallas kernels, late_part(): pl.pallas_call(late_kernel, grid_spec=pltpu.PrefetchScalarGridSpec(num_sc...  6.7 us
  transfers between devices with their start and end apart: 38, of which 21 were waited for; matrix products, arithmetic and copies ran while one was open for 2% of the time, Pallas kernels for 8%

profile of v1, /device:TPU:0, one launch (start us, length us, event | category | flops | bytes accessed | tf_op | source)
XLA Modules:
  0.0 243.8 jit_solution(18297148365939503249)
XLA Ops:
  0.0 3.0 %fusion.10 = (bf16[1024,256]{1,0:T(8,128)(2,1)}, bf16[1024,256]{1,0:T(8,128)(2,1)}, bf16[1024,256]{1,0:T(8,128)(2,1)}, bf16[1024,256]{1,0:T(8,128)(2,1)}) fusion(bf16[4096,256]{1,0:T(8,128)(2,1)} %refs_26_.1), kind=kLoop, calls=%fused_computation.55 | loop fusion | bytes 4194304 | tf_op jit(solution)/shard_map/slice | solution.py:393
  3.0 3.0 %collective-permute-start.21 = (bf16[1024,256]{1,0:T(8,128)(2,1)}, bf16[1024,256]{1,0:T(8,128)(2,1)S(1)}, u32[]{:S(2)}, u32[]{:S(2)}) collective-permute-start(bf16[1024,256]{1,0:T(8,128)(2,1)} %get-tuple-element.42), channel_id=1, source_target_pairs={{1,0},{3,1},{5,3},{7,5},{6,7},{4,6},{2,4},{0,2},{9,8},{11,9},{13,1... | collective-permute-start | bytes 1572872 | tf_op jit(solution)/shard_map/ppermute | solution.py:400
  9.7 5.5 %bath.1 = (bf16[4096,256]{1,0:T(8,128)(2,1)S(1)}, f32[256,256]{1,0:T(8,128)S(1)}) custom-call(s32[8]{0:T(128)S(1)} %copy-done.21, bf16[4,512,512]{2,1,0:T(8,128)(2,1)S(1)} %copy-done.8, bf16[4096,256]{1,0:T(8,128)(2,1)S(1)} %copy-done), custom_call_target="tpu_custom_call" | custom-call | tf_op jit(solution)/shard_map/bath/pallas_call | solution.py:35
  16.5 2.5 %collective-permute-done.21.refs_4_ = bf16[1024,256]{1,0:T(8,128)(2,1)S(1)} collective-permute-done((bf16[1024,256]{1,0:T(8,128)(2,1)}, bf16[1024,256]{1,0:T(8,128)(2,1)S(1)}, u32[]{:S(2)}, u32[]{:S(2)}) %collective-permute-start.21) | collective-permute-done | bytes 524320 | tf_op jit(solution)/shard_map/ppermute | solution.py:400
  19.1 2.2 collective-permute-start.22
  21.3 9.0 %collective-permute-done.14.refs_3_ = bf16[1024,256]{1,0:T(8,128)(2,1)} collective-permute-done((bf16[1024,256]{1,0:T(8,128)(2,1)}, bf16[1024,256]{1,0:T(8,128)(2,1)}, u32[]{:S(2)}, u32[]{:S(2)}) %collective-permute-start.14) | collective-permute-done | bytes 524320 | tf_op jit(solution)/shard_map/ppermute | solution.py:400
  35.4 2.3 collective-permute-done.24
  37.7 3.8 %collective-permute-done.22.refs_8_ = bf16[1024,256]{1,0:T(8,128)(2,1)} collective-permute-done((bf16[1024,256]{1,0:T(8,128)(2,1)S(1)}, bf16[1024,256]{1,0:T(8,128)(2,1)}, u32[]{:S(2)}, u32[]{:S(2)}) %collective-permute-start.22) | collective-permute-done | bytes 524320 | tf_op jit(solution)/shard_map/ppermute | solution.py:400
  41.5 2.1 collective-permute-start.25
  43.7 9.1 %collective-permute-done.15.refs_7_ = bf16[1024,256]{1,0:T(8,128)(2,1)} collective-permute-done((bf16[1024,256]{1,0:T(8,128)(2,1)}, bf16[1024,256]{1,0:T(8,128)(2,1)}, u32[]{:S(2)}, u32[]{:S(2)}) %collective-permute-start.15) | collective-permute-done | bytes 524320 | tf_op jit(solution)/shard_map/ppermute | solution.py:400
  52.7 2.1 collective-permute-start.16
  54.9 9.0 %collective-permute-done.25.refs_12_ = bf16[1024,256]{1,0:T(8,128)(2,1)S(1)} collective-permute-done((bf16[1024,256]{1,0:T(8,128)(2,1)}, bf16[1024,256]{1,0:T(8,128)(2,1)S(1)}, u32[]{:S(2)}, u32[]{:S(2)}) %collective-permute-start.25) | collective-permute-done | bytes 524320 | tf_op jit(solution)/shard_map/ppermute | solution.py:400
  67.6 7.5 %collective-permute-done.16.refs_11_ = bf16[1024,256]{1,0:T(8,128)(2,1)S(1)} collective-permute-done((bf16[1024,256]{1,0:T(8,128)(2,1)}, bf16[1024,256]{1,0:T(8,128)(2,1)S(1)}, u32[]{:S(2)}, u32[]{:S(2)}) %collective-permute-start.16) | collective-permute-done | bytes 524320 | tf_op jit(solution)/shard_map/ppermute | solution.py:400
  78.9 7.6 %collective-permute-done.26.refs_16_ = bf16[1024,256]{1,0:T(8,128)(2,1)} collective-permute-done((bf16[1024,256]{1,0:T(8,128)(2,1)S(1)}, bf16[1024,256]{1,0:T(8,128)(2,1)}, u32[]{:S(2)}, u32[]{:S(2)}) %collective-permute-start.26) | collective-permute-done | bytes 524320 | tf_op jit(solution)/shard_map/ppermute | solution.py:400
  86.5 2.1 collective-permute-start.27
  88.6 9.1 %collective-permute-done.17.refs_15_ = bf16[1024,256]{1,0:T(8,128)(2,1)} collective-permute-done((bf16[1024,256]{1,0:T(8,128)(2,1)S(1)}, bf16[1024,256]{1,0:T(8,128)(2,1)}, u32[]{:S(2)}, u32[]{:S(2)}) %collective-permute-start.17) | collective-permute-done | bytes 524320 | tf_op jit(solution)/shard_map/ppermute | solution.py:400
  97.7 2.1 collective-permute-start.18
  100.2 8.8 %collective-permute-done.27.refs_20_ = bf16[1024,256]{1,0:T(8,128)(2,1)} collective-permute-done((bf16[1024,256]{1,0:T(8,128)(2,1)}, bf16[1024,256]{1,0:T(8,128)(2,1)}, u32[]{:S(2)}, u32[]{:S(2)}) %collective-permute-start.27) | collective-permute-done | bytes 524320 | tf_op jit(solution)/shard_map/ppermute | solution.py:400
  111.1 9.1 %collective-permute-done.18.refs_19_ = bf16[1024,256]{1,0:T(8,128)(2,1)} collective-permute-done((bf16[1024,256]{1,0:T(8,128)(2,1)}, bf16[1024,256]{1,0:T(8,128)(2,1)}, u32[]{:S(2)}, u32[]{:S(2)}) %collective-permute-start.18) | collective-permute-done | bytes 524320 | tf_op jit(solution)/shard_map/ppermute | solution.py:400
  123.8 7.6 %collective-permute-done.28.refs_24_ = bf16[1024,256]{1,0:T(8,128)(2,1)} collective-permute-done((bf16[1024,256]{1,0:T(8,128)(2,1)}, bf16[1024,256]{1,0:T(8,128)(2,1)}, u32[]{:S(2)}, u32[]{:S(2)}) %collective-permute-start.28) | collective-permute-done | bytes 524320 | tf_op jit(solution)/shard_map/ppermute | solution.py:400
  133.6 9.1 %collective-permute-done.19.refs_23_ = bf16[1024,256]{1,0:T(8,128)(2,1)} collective-permute-done((bf16[1024,256]{1,0:T(8,128)(2,1)}, bf16[1024,256]{1,0:T(8,128)(2,1)}, u32[]{:S(2)}, u32[]{:S(2)}) %collective-permute-start.19) | collective-permute-done | bytes 524320 | tf_op jit(solution)/shard_map/ppermute | solution.py:400
  153.8 12.9 %couple_early.1.refs_5_ = f32[4096,256]{1,0:T(8,128)S(1)} custom-call(s32[8,8]{1,0:T(8,128)S(1)} %get-tuple-element.39.origin_ref, s32[8,8]{1,0:T(8,128)S(1)} %get-tuple-element.38.offset_ref, s32[8]{0:T(128)S(1)} %broadcast_in_dim.58.first_ref, s32[8]{0:T(128)S(1)} %sub.84.count_ref.first_ref, s32[8,8]{1,0:T(8,128)S(1)} %get-tuple-element.37.kind_ref, ...), custom_call_target="tpu_custom_call" | custom-call | flops 4294967296 | bytes 16777216 | tf_op jit(solution)/shard_map/couple_early/pallas_call | solution.py:160
  166.7 6.7 %couple_late.1 = (bf16[4096,256]{1,0:T(8,128)(2,1)S(1)}, f32[256,512]{1,0:T(8,128)S(1)}) custom-call(s32[8,8]{1,0:T(8,128)S(1)} %get-tuple-element.39.origin_ref, s32[8,8]{1,0:T(8,128)S(1)} %get-tuple-element.38.offset_ref, s32[8]{0:T(128)S(1)} %sub.84.count_ref.first_ref, s32[8]{0:T(128)S(1)} %get-tuple-element.40.count_ref, ...), custom_call_target="tpu_custom_call" | custom-call | tf_op jit(solution)/shard_map/couple_late/pallas_call | solution.py:195
  177.8 4.0 %collective-permute-start.31 = (f32[64,512]{1,0:T(8,128)S(1)}, f32[64,512]{1,0:T(8,128)S(1)}, u32[]{:S(2)}, u32[]{:S(2)}) collective-permute-start(f32[64,512]{1,0:T(8,128)S(1)} %constant_dynamic-slice_fusion), channel_id=1, source_target_pairs={{0,16},{8,24},{16,0},{24,8},{1,17},{9,25},{17,1},{25,9},{2,18},{10... | collective-permute-start | bytes 393224 | tf_op jit(solution)/shard_map/ppermute | solution.py:442
  181.8 3.8 %collective-permute-done.31 = f32[64,512]{1,0:T(8,128)S(1)} collective-permute-done((f32[64,512]{1,0:T(8,128)S(1)}, f32[64,512]{1,0:T(8,128)S(1)}, u32[]{:S(2)}, u32[]{:S(2)}) %collective-permute-start.31) | collective-permute-done | bytes 131104 | tf_op jit(solution)/shard_map/ppermute | solution.py:442
  186.8 3.6 %collective-permute-done.32 = f32[32,768]{1,0:T(8,128)S(1)} collective-permute-done((f32[32,768]{1,0:T(8,128)S(1)}, f32[32,768]{1,0:T(8,128)S(1)}, u32[]{:S(2)}, u32[]{:S(2)}) %collective-permute-start.32) | collective-permute-done | bytes 98336 | tf_op jit(solution)/shard_map/ppermute | solution.py:442
  190.4 6.1 %collective-permute-start.33 = (f32[32,768]{1,0:T(8,128)S(1)}, f32[32,768]{1,0:T(8,128)S(1)}, u32[]{:S(2)}, u32[]{:S(2)}) collective-permute-start(f32[32,768]{1,0:T(8,128)S(1)} %fusion.2), channel_id=1, source_target_pairs={{0,2},{1,3},{2,0},{3,1},{4,6},{5,7},{6,4},{7,5},{8,10},{9,11},{10,... | collective-permute-start | bytes 294920 | tf_op jit(solution)/shard_map/ppermute | solution.py:442
  196.4 3.1 %collective-permute-done.33 = f32[32,768]{1,0:T(8,128)S(1)} collective-permute-done((f32[32,768]{1,0:T(8,128)S(1)}, f32[32,768]{1,0:T(8,128)S(1)}, u32[]{:S(2)}, u32[]{:S(2)}) %collective-permute-start.33) | collective-permute-done | bytes 98336 | tf_op jit(solution)/shard_map/ppermute | solution.py:442
  200.0 5.1 %collective-permute-done.34 = f32[32,768]{1,0:T(8,128)S(1)} collective-permute-done((f32[32,768]{1,0:T(8,128)S(1)}, f32[32,768]{1,0:T(8,128)S(1)}, u32[]{:S(2)}, u32[]{:S(2)}) %collective-permute-start.34) | collective-permute-done | bytes 98336 | tf_op jit(solution)/shard_map/ppermute | solution.py:442
  206.9 2.9 %collective-permute-done.35 = f32[32,768]{1,0:T(8,128)S(1)} collective-permute-done((f32[32,768]{1,0:T(8,128)S(1)}, f32[32,768]{1,0:T(8,128)S(1)}, u32[]{:S(2)}, u32[]{:S(2)}) %collective-permute-start.35) | collective-permute-done | bytes 98336 | tf_op jit(solution)/shard_map/ppermute | solution.py:442
  211.3 4.2 %collective-permute-done.36 = f32[64,768]{1,0:T(8,128)S(1)} collective-permute-done((f32[64,768]{1,0:T(8,128)S(1)}, f32[64,768]{1,0:T(8,128)S(1)}, u32[]{:S(2)}, u32[]{:S(2)}) %collective-permute-start.36) | collective-permute-done | bytes 196640 | tf_op jit(solution)/shard_map/ppermute | solution.py:442
  219.0 24.6 %finish.1 = bf16[4096,256]{1,0:T(8,128)(2,1)} custom-call(s32[8]{0:T(128)S(1)} %stack.35.order_ref, f32[256,768]{1,0:T(8,128)S(1)} %pad_maximum_fusion.chunks_ref, bf16[4096,256]{1,0:T(8,128)(2,1)S(1)} %copy-done.7, bf16[4096,256]{1,0:T(8,128)(2,1)S(1)} %copy-done.3), custom_call_target="tpu_custom_call" | custom-call | tf_op jit(solution)/shard_map/finish/pallas_call | solution.py:343
  (127 shorter events, 50.0 us)
Async XLA Ops:
  3.0 15.9 %collective-permute-start.21 = (bf16[1024,256]{1,0:T(8,128)(2,1)}, bf16[1024,256]{1,0:T(8,128)(2,1)S(1)}, u32[]{:S(2)}, u32[]{:S(2)}) collective-permute-start(bf16[1024,256]{1,0:T(8,128)(2,1)} %get-tuple-element.42), channel_id=1, source_target_pairs={{1,0},{3,1},{5,3},{7,5},{6,7},{4,6},{2,4},{0,2},{9,8},{11,9},{13,1... | collective-permute-start | bytes 1572872 | tf_op jit(solution)/shard_map/ppermute | solution.py:400
  6.0 15.2 %collective-permute-start.7 = (bf16[1024,256]{1,0:T(8,128)(2,1)}, bf16[1024,256]{1,0:T(8,128)(2,1)S(1)}, u32[]{:S(2)}, u32[]{:S(2)}) collective-permute-start(bf16[1024,256]{1,0:T(8,128)(2,1)} %get-tuple-element.44), channel_id=1, source_target_pairs={{0,1},{1,3},{3,5},{5,7},{7,6},{6,4},{4,2},{2,0},{8,9},{9,11},{11,1... | collective-permute-start | bytes 1572872 | tf_op jit(solution)/shard_map/ppermute | solution.py:400
  6.0 24.2 %collective-permute-start.14 = (bf16[1024,256]{1,0:T(8,128)(2,1)}, bf16[1024,256]{1,0:T(8,128)(2,1)}, u32[]{:S(2)}, u32[]{:S(2)}) collective-permute-start(bf16[1024,256]{1,0:T(8,128)(2,1)} %get-tuple-element.43), channel_id=1, source_target_pairs={{1,0},{3,1},{5,3},{7,5},{6,7},{4,6},{2,4},{0,2},{9,8},{11,9},{13,1... | collective-permute-start | bytes 1572872 | tf_op jit(solution)/shard_map/ppermute | solution.py:400
  8.1 24.4 %collective-permute-start = (bf16[1024,256]{1,0:T(8,128)(2,1)}, bf16[1024,256]{1,0:T(8,128)(2,1)}, u32[]{:S(2)}, u32[]{:S(2)}) collective-permute-start(bf16[1024,256]{1,0:T(8,128)(2,1)} %get-tuple-element.45), channel_id=1, source_target_pairs={{0,1},{1,3},{3,5},{5,7},{7,6},{6,4},{4,2},{2,0},{8,9},{9,11},{11,1... | collective-permute-start | bytes 1572872 | tf_op jit(solution)/shard_map/ppermute | solution.py:400
  18.9 13.5 %collective-permute-start.23 = (f32[128,256]{1,0:T(8,128)S(1)}, f32[128,256]{1,0:T(8,128)}, u32[]{:S(2)}, u32[]{:S(2)}) collective-permute-start(f32[128,256]{1,0:T(8,128)S(1)} %constant_dynamic-slice_fusion.3), channel_id=1, source_target_pairs={{0,8},{8,0},{16,24},{24,16},{1,9},{9,1},{17,25},{25,17},{2,10},{10... | collective-permute-start | bytes 393224 | tf_op jit(solution)/shard_map/ppermute | solution.py:442
  19.1 22.4 %collective-permute-start.22 = (bf16[1024,256]{1,0:T(8,128)(2,1)S(1)}, bf16[1024,256]{1,0:T(8,128)(2,1)}, u32[]{:S(2)}, u32[]{:S(2)}) collective-permute-start(bf16[1024,256]{1,0:T(8,128)(2,1)S(1)} %collective-permute-done.21.refs_4_), channel_id=1, source_target_pairs={{1,0},{3,1},{5,3},{7,5},{6,7},{4,6},{2,4},{0,2},{9,8},{11,9},{13,1... | collective-permute-start | bytes 1572872 | tf_op jit(solution)/shard_map/ppermute | solution.py:400
  21.2 22.4 %collective-permute-start.8 = (bf16[1024,256]{1,0:T(8,128)(2,1)S(1)}, bf16[1024,256]{1,0:T(8,128)(2,1)}, u32[]{:S(2)}, u32[]{:S(2)}) collective-permute-start(bf16[1024,256]{1,0:T(8,128)(2,1)S(1)} %collective-permute-done.7.refs_2_), channel_id=1, source_target_pairs={{0,1},{1,3},{3,5},{5,7},{7,6},{6,4},{4,2},{2,0},{8,9},{9,11},{11,1... | collective-permute-start | bytes 1572872 | tf_op jit(solution)/shard_map/ppermute | solution.py:400
  30.3 22.5 %collective-permute-start.15 = (bf16[1024,256]{1,0:T(8,128)(2,1)}, bf16[1024,256]{1,0:T(8,128)(2,1)}, u32[]{:S(2)}, u32[]{:S(2)}) collective-permute-start(bf16[1024,256]{1,0:T(8,128)(2,1)} %collective-permute-done.14.refs_3_), channel_id=1, source_target_pairs={{1,0},{3,1},{5,3},{7,5},{6,7},{4,6},{2,4},{0,2},{9,8},{11,9},{13,1... | collective-permute-start | bytes 1572872 | tf_op jit(solution)/shard_map/ppermute | solution.py:400
  32.4 22.5 %collective-permute-start.1 = (bf16[1024,256]{1,0:T(8,128)(2,1)}, bf16[1024,256]{1,0:T(8,128)(2,1)}, u32[]{:S(2)}, u32[]{:S(2)}) collective-permute-start(bf16[1024,256]{1,0:T(8,128)(2,1)} %collective-permute-done.refs_1_), channel_id=1, source_target_pairs={{0,1},{1,3},{3,5},{5,7},{7,6},{6,4},{4,2},{2,0},{8,9},{9,11},{11,1... | collective-permute-start | bytes 1572872 | tf_op jit(solution)/shard_map/ppermute | solution.py:400
  41.5 22.4 %collective-permute-start.25 = (bf16[1024,256]{1,0:T(8,128)(2,1)}, bf16[1024,256]{1,0:T(8,128)(2,1)S(1)}, u32[]{:S(2)}, u32[]{:S(2)}) collective-permute-start(bf16[1024,256]{1,0:T(8,128)(2,1)} %collective-permute-done.22.refs_8_), channel_id=1, source_target_pairs={{1,0},{3,1},{5,3},{7,5},{6,7},{4,6},{2,4},{0,2},{9,8},{11,9},{13,1... | collective-permute-start | bytes 1572872 | tf_op jit(solution)/shard_map/ppermute | solution.py:400
  43.7 23.1 %collective-permute-start.9 = (bf16[1024,256]{1,0:T(8,128)(2,1)}, bf16[1024,256]{1,0:T(8,128)(2,1)S(1)}, u32[]{:S(2)}, u32[]{:S(2)}) collective-permute-start(bf16[1024,256]{1,0:T(8,128)(2,1)} %collective-permute-done.8.refs_6_), channel_id=1, source_target_pairs={{0,1},{1,3},{3,5},{5,7},{7,6},{6,4},{4,2},{2,0},{8,9},{9,11},{11,1... | collective-permute-start | bytes 1572872 | tf_op jit(solution)/shard_map/ppermute | solution.py:400
  52.7 22.4 %collective-permute-start.16 = (bf16[1024,256]{1,0:T(8,128)(2,1)}, bf16[1024,256]{1,0:T(8,128)(2,1)S(1)}, u32[]{:S(2)}, u32[]{:S(2)}) collective-permute-start(bf16[1024,256]{1,0:T(8,128)(2,1)} %collective-permute-done.15.refs_7_), channel_id=1, source_target_pairs={{1,0},{3,1},{5,3},{7,5},{6,7},{4,6},{2,4},{0,2},{9,8},{11,9},{13,1... | collective-permute-start | bytes 1572872 | tf_op jit(solution)/shard_map/ppermute | solution.py:400
  54.9 23.1 %collective-permute-start.2 = (bf16[1024,256]{1,0:T(8,128)(2,1)}, bf16[1024,256]{1,0:T(8,128)(2,1)S(1)}, u32[]{:S(2)}, u32[]{:S(2)}) collective-permute-start(bf16[1024,256]{1,0:T(8,128)(2,1)} %collective-permute-done.1.refs_5_), channel_id=1, source_target_pairs={{0,1},{1,3},{3,5},{5,7},{7,6},{6,4},{4,2},{2,0},{8,9},{9,11},{11,1... | collective-permute-start | bytes 1572872 | tf_op jit(solution)/shard_map/ppermute | solution.py:400
  63.9 22.6 %collective-permute-start.26 = (bf16[1024,256]{1,0:T(8,128)(2,1)S(1)}, bf16[1024,256]{1,0:T(8,128)(2,1)}, u32[]{:S(2)}, u32[]{:S(2)}) collective-permute-start(bf16[1024,256]{1,0:T(8,128)(2,1)S(1)} %collective-permute-done.25.refs_12_), channel_id=1, source_target_pairs={{1,0},{3,1},{5,3},{7,5},{6,7},{4,6},{2,4},{0,2},{9,8},{11,9},{13,1... | collective-permute-start | bytes 1572872 | tf_op jit(solution)/shard_map/ppermute | solution.py:400
  66.8 21.8 %collective-permute-start.10 = (bf16[1024,256]{1,0:T(8,128)(2,1)S(1)}, bf16[1024,256]{1,0:T(8,128)(2,1)}, u32[]{:S(2)}, u32[]{:S(2)}) collective-permute-start(bf16[1024,256]{1,0:T(8,128)(2,1)S(1)} %collective-permute-done.9.refs_10_), channel_id=1, source_target_pairs={{0,1},{1,3},{3,5},{5,7},{7,6},{6,4},{4,2},{2,0},{8,9},{9,11},{11,1... | collective-permute-start | bytes 1572872 | tf_op jit(solution)/shard_map/ppermute | solution.py:400
  75.1 22.6 %collective-permute-start.17 = (bf16[1024,256]{1,0:T(8,128)(2,1)S(1)}, bf16[1024,256]{1,0:T(8,128)(2,1)}, u32[]{:S(2)}, u32[]{:S(2)}) collective-permute-start(bf16[1024,256]{1,0:T(8,128)(2,1)S(1)} %collective-permute-done.16.refs_11_), channel_id=1, source_target_pairs={{1,0},{3,1},{5,3},{7,5},{6,7},{4,6},{2,4},{0,2},{9,8},{11,9},{13,1... | collective-permute-start | bytes 1572872 | tf_op jit(solution)/shard_map/ppermute | solution.py:400
  78.0 21.8 %collective-permute-start.3 = (bf16[1024,256]{1,0:T(8,128)(2,1)S(1)}, bf16[1024,256]{1,0:T(8,128)(2,1)}, u32[]{:S(2)}, u32[]{:S(2)}) collective-permute-start(bf16[1024,256]{1,0:T(8,128)(2,1)S(1)} %collective-permute-done.2.refs_9_), channel_id=1, source_target_pairs={{0,1},{1,3},{3,5},{5,7},{7,6},{6,4},{4,2},{2,0},{8,9},{9,11},{11,1... | collective-permute-start | bytes 1572872 | tf_op jit(solution)/shard_map/ppermute | solution.py:400
  86.5 22.5 %collective-permute-start.27 = (bf16[1024,256]{1,0:T(8,128)(2,1)}, bf16[1024,256]{1,0:T(8,128)(2,1)}, u32[]{:S(2)}, u32[]{:S(2)}) collective-permute-start(bf16[1024,256]{1,0:T(8,128)(2,1)} %collective-permute-done.26.refs_16_), channel_id=1, source_target_pairs={{1,0},{3,1},{5,3},{7,5},{6,7},{4,6},{2,4},{0,2},{9,8},{11,9},{13,1... | collective-permute-start | bytes 1572872 | tf_op jit(solution)/shard_map/ppermute | solution.py:400
  88.6 22.5 %collective-permute-start.11 = (bf16[1024,256]{1,0:T(8,128)(2,1)}, bf16[1024,256]{1,0:T(8,128)(2,1)}, u32[]{:S(2)}, u32[]{:S(2)}) collective-permute-start(bf16[1024,256]{1,0:T(8,128)(2,1)} %collective-permute-done.10.refs_14_), channel_id=1, source_target_pairs={{0,1},{1,3},{3,5},{5,7},{7,6},{6,4},{4,2},{2,0},{8,9},{9,11},{11,1... | collective-permute-start | bytes 1572872 | tf_op jit(solution)/shard_map/ppermute | solution.py:400
  97.7 22.5 %collective-permute-start.18 = (bf16[1024,256]{1,0:T(8,128)(2,1)}, bf16[1024,256]{1,0:T(8,128)(2,1)}, u32[]{:S(2)}, u32[]{:S(2)}) collective-permute-start(bf16[1024,256]{1,0:T(8,128)(2,1)} %collective-permute-done.17.refs_15_), channel_id=1, source_target_pairs={{1,0},{3,1},{5,3},{7,5},{6,7},{4,6},{2,4},{0,2},{9,8},{11,9},{13,1... | collective-permute-start | bytes 1572872 | tf_op jit(solution)/shard_map/ppermute | solution.py:400
  99.8 22.5 %collective-permute-start.4 = (bf16[1024,256]{1,0:T(8,128)(2,1)}, bf16[1024,256]{1,0:T(8,128)(2,1)}, u32[]{:S(2)}, u32[]{:S(2)}) collective-permute-start(bf16[1024,256]{1,0:T(8,128)(2,1)} %collective-permute-done.3.refs_13_), channel_id=1, source_target_pairs={{0,1},{1,3},{3,5},{5,7},{7,6},{6,4},{4,2},{2,0},{8,9},{9,11},{11,1... | collective-permute-start | bytes 1572872 | tf_op jit(solution)/shard_map/ppermute | solution.py:400
  108.9 22.5 %collective-permute-start.28 = (bf16[1024,256]{1,0:T(8,128)(2,1)}, bf16[1024,256]{1,0:T(8,128)(2,1)}, u32[]{:S(2)}, u32[]{:S(2)}) collective-permute-start(bf16[1024,256]{1,0:T(8,128)(2,1)} %collective-permute-done.27.refs_20_), channel_id=1, source_target_pairs={{1,0},{3,1},{5,3},{7,5},{6,7},{4,6},{2,4},{0,2},{9,8},{11,9},{13,1... | collective-permute-start | bytes 1572872 | tf_op jit(solution)/shard_map/ppermute | solution.py:400
  111.1 22.5 %collective-permute-start.12 = (bf16[1024,256]{1,0:T(8,128)(2,1)}, bf16[1024,256]{1,0:T(8,128)(2,1)}, u32[]{:S(2)}, u32[]{:S(2)}) collective-permute-start(bf16[1024,256]{1,0:T(8,128)(2,1)} %collective-permute-done.11.refs_18_), channel_id=1, source_target_pairs={{0,1},{1,3},{3,5},{5,7},{7,6},{6,4},{4,2},{2,0},{8,9},{9,11},{11,1... | collective-permute-start | bytes 1572872 | tf_op jit(solution)/shard_map/ppermute | solution.py:400
  120.2 22.5 %collective-permute-start.19 = (bf16[1024,256]{1,0:T(8,128)(2,1)}, bf16[1024,256]{1,0:T(8,128)(2,1)}, u32[]{:S(2)}, u32[]{:S(2)}) collective-permute-start(bf16[1024,256]{1,0:T(8,128)(2,1)} %collective-permute-done.18.refs_19_), channel_id=1, source_target_pairs={{1,0},{3,1},{5,3},{7,5},{6,7},{4,6},{2,4},{0,2},{9,8},{11,9},{13,1... | collective-permute-start | bytes 1572872 | tf_op jit(solution)/shard_map/ppermute | solution.py:400
  122.3 22.5 %collective-permute-start.5 = (bf16[1024,256]{1,0:T(8,128)(2,1)}, bf16[1024,256]{1,0:T(8,128)(2,1)}, u32[]{:S(2)}, u32[]{:S(2)}) collective-permute-start(bf16[1024,256]{1,0:T(8,128)(2,1)} %collective-permute-done.4.refs_17_), channel_id=1, source_target_pairs={{0,1},{1,3},{3,5},{5,7},{7,6},{6,4},{4,2},{2,0},{8,9},{9,11},{11,1... | collective-permute-start | bytes 1572872 | tf_op jit(solution)/shard_map/ppermute | solution.py:400
  131.4 35.3 %collective-permute-start.29 = (bf16[1024,256]{1,0:T(8,128)(2,1)}, bf16[1024,256]{1,0:T(8,128)(2,1)S(1)}, u32[]{:S(2)}, u32[]{:S(2)}) collective-permute-start(bf16[1024,256]{1,0:T(8,128)(2,1)} %collective-permute-done.28.refs_24_), channel_id=1, source_target_pairs={{1,0},{3,1},{5,3},{7,5},{6,7},{4,6},{2,4},{0,2},{9,8},{11,9},{13,1... | collective-permute-start | bytes 1572872 | tf_op jit(solution)/shard_map/ppermute | solution.py:400
  133.6 33.1 %collective-permute-start.13 = (bf16[1024,256]{1,0:T(8,128)(2,1)}, bf16[1024,256]{1,0:T(8,128)(2,1)S(1)}, u32[]{:S(2)}, u32[]{:S(2)}) collective-permute-start(bf16[1024,256]{1,0:T(8,128)(2,1)} %collective-permute-done.12.refs_22_), channel_id=1, source_target_pairs={{0,1},{1,3},{3,5},{5,7},{7,6},{6,4},{4,2},{2,0},{8,9},{9,11},{11,1... | collective-permute-start | bytes 1572872 | tf_op jit(solution)/shard_map/ppermute | solution.py:400
  142.6 24.0 %collective-permute-start.20 = (bf16[1024,256]{1,0:T(8,128)(2,1)}, bf16[1024,256]{1,0:T(8,128)(2,1)}, u32[]{:S(2)}, u32[]{:S(2)}) collective-permute-start(bf16[1024,256]{1,0:T(8,128)(2,1)} %collective-permute-done.19.refs_23_), channel_id=1, source_target_pairs={{1,0},{3,1},{5,3},{7,5},{6,7},{4,6},{2,4},{0,2},{9,8},{11,9},{13,1... | collective-permute-start | bytes 1572872 | tf_op jit(solution)/shard_map/ppermute | solution.py:400
  144.8 21.9 %collective-permute-start.6 = (bf16[1024,256]{1,0:T(8,128)(2,1)}, bf16[1024,256]{1,0:T(8,128)(2,1)}, u32[]{:S(2)}, u32[]{:S(2)}) collective-permute-start(bf16[1024,256]{1,0:T(8,128)(2,1)} %collective-permute-done.5.refs_21_), channel_id=1, source_target_pairs={{0,1},{1,3},{3,5},{5,7},{7,6},{6,4},{4,2},{2,0},{8,9},{9,11},{11,1... | collective-permute-start | bytes 1572872 | tf_op jit(solution)/shard_map/ppermute | solution.py:400
  177.8 7.8 %collective-permute-start.31 = (f32[64,512]{1,0:T(8,128)S(1)}, f32[64,512]{1,0:T(8,128)S(1)}, u32[]{:S(2)}, u32[]{:S(2)}) collective-permute-start(f32[64,512]{1,0:T(8,128)S(1)} %constant_dynamic-slice_fusion), channel_id=1, source_target_pairs={{0,16},{8,24},{16,0},{24,8},{1,17},{9,25},{17,1},{25,9},{2,18},{10... | collective-permute-start | bytes 393224 | tf_op jit(solution)/shard_map/ppermute | solution.py:442
  190.4 9.1 %collective-permute-start.33 = (f32[32,768]{1,0:T(8,128)S(1)}, f32[32,768]{1,0:T(8,128)S(1)}, u32[]{:S(2)}, u32[]{:S(2)}) collective-permute-start(f32[32,768]{1,0:T(8,128)S(1)} %fusion.2), channel_id=1, source_target_pairs={{0,2},{1,3},{2,0},{3,1},{4,6},{5,7},{6,4},{7,5},{8,10},{9,11},{10,... | collective-permute-start | bytes 294920 | tf_op jit(solution)/shard_map/ppermute | solution.py:442
  209.8 5.7 %collective-permute-start.36 = (f32[64,768]{1,0:T(8,128)S(1)}, f32[64,768]{1,0:T(8,128)S(1)}, u32[]{:S(2)}, u32[]{:S(2)}) collective-permute-start(f32[64,768]{1,0:T(8,128)S(1)} %pad_maximum_fusion.2), channel_id=1, source_target_pairs={{0,16},{8,24},{16,0},{24,8},{1,17},{9,25},{17,1},{25,9},{2,18},{10... | collective-permute-start | bytes 589832 | tf_op jit(solution)/shard_map/ppermute | solution.py:442
  (32 other events, 761.7 us)
